TPU v7x, 32 devices: a whole 2x2x4 slice. The times are simulated.
32 devices in a mesh: tm: 4 (over y, core), space: 8 (over z, x).
Axes of the slice: x: 2, y: 2, z: 4, core: 2. Of those that a mesh axis runs over, the one named last changes fastest.
Arguments:
- init_states: float32 [2, 4, 256, 16, 128], P(None, 'tm', None, 'space'), may hold values from -6 to 6
- forcing: float32 [2, 256, 16, 128], P(None, None, 'space'), may hold values from -6 to 6
- damp: float32 [2, 256, 16, 128], P(None, None, 'space'), may hold values from 0.3 to 0.95
- kappa_x: float32 [256], replicated, may hold values from 2 to 60
- kappa_y: float32 [16], replicated, may hold values from 2 to 60
- kappa_z: float32 [128], replicated, may hold values from 0.02 to 0.24
- sea_tiles: int32 [16, 1], replicated, may hold values 0 or 1
- phases: int32 [4], P('tm'), may hold values from 0 to 11
Outputs:
- slab_starts: float32 [2, 4, 256, 16, 128], P(None, 'tm', None, 'space')
All inputs are finite; a program needn't handle non-finite values.
Results may differ from a plain program's by a relative error of at most 0.0003.
Values sent between devices are 32-bit elements; how exact they have to be, the bound alone decides.
A program may use at most 64 MiB of HBM per device.

v0:
```python
import functools
import math

import jax
import jax.numpy as jnp
from jax import lax
from jax.experimental import pallas as pl
from jax.experimental.pallas import tpu as pltpu
from jax.sharding import PartitionSpec as P

STEPS = 2
ITERS = 2
TILE = 16
PHASES = 12


def shifted(array, axis, by):
    devices = lax.axis_size(axis)
    return lax.ppermute(array, axis, [(i, (i + by) % devices) for i in range(devices)])


def line_inverse(kappa):
    face = 0.5 * (kappa[1:] + kappa[:-1])
    zero = jnp.zeros((1,), kappa.dtype)
    left = jnp.concatenate([zero, face])
    right = jnp.concatenate([face, zero])
    identity = jnp.eye(kappa.shape[0], dtype=kappa.dtype)
    return lax.linalg.tridiagonal_solve(-left, 1.0 + left + right, -right, identity)


def solve_lines(field, inverse):
    return jnp.matmul(inverse, field, precision=lax.Precision.HIGHEST)


def solve_x(field, inverse):
    shape = field.shape
    flat = field.reshape(shape[0], shape[1], shape[2], shape[3] * shape[4])
    return solve_lines(flat, inverse).reshape(shape)


def vertical_mix(field, kappa_z):
    face = 0.5 * (kappa_z[1:] + kappa_z[:-1])
    flux = face * (field[..., 1:] - field[..., :-1])
    zeros = jnp.zeros(field.shape[:-1] + (1,), field.dtype)
    flux = jnp.concatenate([zeros, flux, zeros], axis=-1)
    return field + flux[..., 1:] - flux[..., :-1]


def compose(earlier, later):
    return (earlier[0] * later[0], later[0] * earlier[1] + later[1])


def column_pass(field, inverse_y):
    return lax.all_to_all(
        solve_lines(
            lax.all_to_all(field, "space", split_axis=2, concat_axis=3, tiled=True), inverse_y
        ),
        "space",
        split_axis=3,
        concat_axis=2,
        tiled=True,
    )


def body(init_states, forcing, damp, kappa_x, kappa_y, kappa_z, sea_tiles, phases):
    row_count = init_states.shape[3]
    inverse_x = line_inverse(kappa_x)
    inverse_y = line_inverse(kappa_y)
    tiles = sea_tiles.astype(jnp.float32)
    sea = jnp.repeat(jnp.repeat(tiles, TILE, axis=0), TILE, axis=1)
    sea_rows = lax.dynamic_slice_in_dim(sea, lax.axis_index("space") * row_count, row_count, 1)
    source = (forcing * sea_rows[None, :, :, None])[:, None]
    phase_float = phases.astype(jnp.float32)
    weight = 1.0 + 0.5 * jnp.cos(2.0 * math.pi * phase_float / PHASES)
    factors = jnp.exp(weight[None, :, None, None, None] * jnp.log(damp)[:, None])
    states = init_states
    for iteration in range(ITERS):
        field = states
        for step in range(STEPS):
            amplitude = jnp.cos(2.0 * math.pi * (phase_float * STEPS + step) / (PHASES * STEPS))[
                None, :, None, None, None
            ]
            if step % 2 == 0:
                field = column_pass(solve_x(field, inverse_x), inverse_y)
            else:
                field = solve_x(column_pass(field, inverse_y), inverse_x)
            field = vertical_mix(field, kappa_z) + amplitude * source
        offsets = field - factors * states
        own_factor = factors[:, 0]
        own_offset = offsets[:, 0]
        own = (own_factor, own_offset)
        ident = (jnp.ones_like(own_factor), jnp.zeros_like(own_offset))
        count = lax.axis_size("tm")
        here = lax.axis_index("tm")
        lower_part = ident
        upper_part = ident
        moving = jnp.stack([own_factor, own_offset])
        for turn in range(1, count):
            moving = shifted(moving, "tm", 1)
            piece = (moving[0], moving[1])
            anchor = (here - turn) % count
            before = anchor < here
            joined_low = compose(piece, lower_part)
            joined_high = compose(piece, upper_part)
            lower_part = (
                jnp.where(before, joined_low[0], lower_part[0]),
                jnp.where(before, joined_low[1], lower_part[1]),
            )
            upper_part = (
                jnp.where(before, upper_part[0], joined_high[0]),
                jnp.where(before, upper_part[1], joined_high[1]),
            )
        period = compose(compose(lower_part, own), upper_part)
        first = period[1] / (1.0 - period[0])
        start = lower_part[0] * first + lower_part[1]
        fresh = [start]
        states = jnp.stack(fresh, axis=1)
    return states


LANES = 128
HALO = 2 * ITERS
MESH = pl.DeviceIdType.MESH


def dot(a, b):
    return jnp.dot(a, b, precision=lax.Precision.HIGHEST, preferred_element_type=jnp.float32)


def parts(a):
    high = a.astype(jnp.bfloat16)
    return high, (a - high.astype(jnp.float32)).astype(jnp.bfloat16)


def dot3(a, b):
    once = functools.partial(jnp.dot, preferred_element_type=jnp.float32)
    return once(a[0], b[0]) + (once(a[0], b[1]) + once(a[1], b[0]))


def iota(shape, axis):
    return lax.broadcasted_iota(jnp.int32, shape, axis)


def faces(kappa_row, n):
    row, col = iota((n, n), 0), iota((n, n), 1)
    own = jnp.sum(jnp.where(row == col, kappa_row, 0.0), axis=1, keepdims=True)
    face = 0.5 * (own + kappa_row)
    below = jnp.where(col == row - 1, face, 0.0)
    above = jnp.where(col == row + 1, face, 0.0)
    return (
        jnp.sum(below, axis=1, keepdims=True),
        jnp.sum(above, axis=1, keepdims=True),
        below + above,
    )


def reduced_inverse(kappa_row, n):
    lower, upper, _ = faces(kappa_row, n)
    shape = (n, LANES)
    a = jnp.broadcast_to(-lower, shape)
    c = jnp.broadcast_to(-upper, shape)
    b = 1.0 - a - c
    blocks = [
        (iota(shape, 0) == iota(shape, 1) + LANES * j).astype(jnp.float32)
        for j in range(max(n // LANES, 1))
    ]
    s = 1
    while s < n:
        before = functools.partial(pltpu.roll, shift=s, axis=0)
        after = functools.partial(pltpu.roll, shift=n - s, axis=0)
        alpha = -a / before(b)
        gamma = -c / after(b)
        blocks = [d + alpha * before(d) + gamma * after(d) for d in blocks]
        b = b + alpha * before(c) + gamma * after(a)
        a, c = alpha * before(a), gamma * after(c)
        s *= 2
    inverse = 1.0 / b
    return [d * inverse for d in blocks]


def period_kernel(
    size, u_hbm, f_hbm, damp_hbm, kx_hbm, ky_hbm, kz_hbm, sea_hbm, phase_ref, out_ref,
    u_ref, f_ref, damp_ref, kx_ref, ky_ref, kz_ref, sea_ref, fetched, inverse_p, split, ends,
    ubuf, fbuf, pbuf, xbuf, dbuf, qbuf, obuf, rbuf, g_ref, a_ref, state, factor, source, offset_ref,
    u_send, u_recv, f_send, f_recv, p_send, p_recv, o_send, o_recv,
):
    n_tm, n_sp, n_t, nx, rows, nz = size
    count = n_tm * n_sp
    per = count // n_t
    chunk = nz // per
    window = chunk + 2 * HALO
    halves = nx // LANES
    wrows = window * rows
    crows = chunk * rows
    all_rows = n_sp * wrows
    ny = n_sp * rows

    here = lax.axis_index("tm")
    spot = lax.axis_index("space")
    me = here * n_sp + spot

    def window_start(k):
        return jnp.minimum(jnp.maximum(k * chunk - HALO, 0), nz - window)

    def window_rows(k):
        return pl.ds(pl.multiple_of(window_start(k) * rows, 8), wrows)

    def chunk_rows(k):
        return pl.ds(pl.multiple_of(k * crows, 8), crows)

    def device(index):
        return {"tm": index // n_sp, "space": index % n_sp}

    pairs = (
        (damp_hbm, damp_ref),
        (f_hbm, f_ref),
        (u_hbm, u_ref),
        (kx_hbm, kx_ref),
        (ky_hbm, ky_ref),
        (kz_hbm, kz_ref),
        (sea_hbm, sea_ref),
    )
    fetches = [
        pltpu.make_async_copy(far, near, fetched.at[i]) for i, (far, near) in enumerate(pairs)
    ]
    for fetch in fetches:
        fetch.start()

    barrier = pltpu.get_barrier_semaphore()

    @pl.loop(1, count)
    def greet(offset):
        pl.semaphore_signal(
            barrier, inc=1, device_id=device((me + offset) % count), device_id_type=MESH
        )

    def turn(ref, buf, where):
        for t in range(n_t):
            for half in range(halves):
                for y in range(rows):
                    part = ref[t, pl.ds(half * LANES * rows + y, LANES, stride=rows), :]
                    buf[(t, *where, half, pl.ds(y, nz, stride=rows), slice(None))] = part.T

    pbuf[...] = jnp.full((8, LANES), phase_ref[0].astype(jnp.float32))

    my_t, my_k = me // per, me % per
    my_start = window_start(my_k)

    own_copies = [
        pltpu.make_async_copy(
            ubuf.at[my_t, :, window_rows(my_k), :], xbuf.at[here, spot], u_recv.at[me]
        ),
        pltpu.make_async_copy(
            fbuf.at[my_t, :, :, window_rows(my_k), :], dbuf.at[spot], f_recv.at[spot]
        ),
        pltpu.make_async_copy(pbuf, qbuf.at[here], p_recv.at[here]),
    ]

    def send_u(offset):
        index = (me + offset) % count
        return pltpu.make_async_remote_copy(
            src_ref=ubuf.at[index // per, :, window_rows(index % per), :],
            dst_ref=xbuf.at[here, spot],
            send_sem=u_send.at[offset],
            recv_sem=u_recv.at[me],
            device_id=device(index),
            device_id_type=MESH,
        )

    def send_f(offset):
        index = here * n_sp + (spot + offset) % n_sp
        return pltpu.make_async_remote_copy(
            src_ref=fbuf.at[index // per, :, :, window_rows(index % per), :],
            dst_ref=dbuf.at[spot],
            send_sem=f_send.at[offset],
            recv_sem=f_recv.at[spot],
            device_id=device(index),
            device_id_type=MESH,
        )

    def send_p(offset):
        return pltpu.make_async_remote_copy(
            src_ref=pbuf,
            dst_ref=qbuf.at[here],
            send_sem=p_send.at[offset],
            recv_sem=p_recv.at[here],
            device_id={"tm": (here + offset) % n_tm, "space": spot},
            device_id_type=MESH,
        )

    def send_o(index):
        inner = pl.multiple_of((my_k * chunk - my_start) * rows, 8)
        return pltpu.make_async_remote_copy(
            src_ref=obuf.at[index // n_sp, index % n_sp, :, pl.ds(inner, crows), :],
            dst_ref=rbuf.at[my_t, :, chunk_rows(my_k), :],
            send_sem=o_send.at[index],
            recv_sem=o_recv.at[me],
            device_id=device(index),
            device_id_type=MESH,
        )

    fetches[0].wait()
    turn(damp_ref, fbuf, (0,))
    fetches[1].wait()
    turn(f_ref, fbuf, (1,))
    pl.semaphore_wait(barrier, count - 1)

    @pl.loop(1, n_tm)
    def start_p(offset):
        send_p(offset).start()

    @pl.loop(1, n_sp)
    def start_f(offset):
        send_f(offset).start()

    own_copies[1].start()
    own_copies[2].start()
    fetches[2].wait()
    turn(u_ref, ubuf, ())

    @pl.loop(1, count)
    def start_u(offset):
        send_u(offset).start()

    own_copies[0].start()
    for fetch in fetches[3:]:
        fetch.wait()

    for half, block in enumerate(reduced_inverse(kx_ref[...], nx)):
        a_ref[0, :, half * LANES : (half + 1) * LANES] = block
    a_ref[1] = dot(a_ref[0], a_ref[0])
    q, j = iota((all_rows, ny), 0), iota((all_rows, ny), 1)
    line = (q // wrows) * rows + q % rows
    pick_y = (line == j).astype(jnp.float32)
    q, j = iota((LANES, all_rows), 1), iota((LANES, all_rows), 0)
    line = (q // wrows) * rows + q % rows
    pick_y_back = (line == j).astype(jnp.float32)
    big_y = dot(dot(pick_y, reduced_inverse(ky_ref[...], ny)[0]), pick_y_back)
    _, _, beside = faces(kz_ref[...], nz)
    identity = (iota((nz, nz), 0) == iota((nz, nz), 1)).astype(jnp.float32)
    vertical = beside + identity * (1.0 - jnp.sum(beside, axis=1, keepdims=True))
    q, j = iota((all_rows, nz), 0), iota((all_rows, nz), 1)
    pick_z = (my_start + (q % wrows) // rows == j).astype(jnp.float32)
    q, j = iota((nz, all_rows), 1), iota((nz, all_rows), 0)
    pick_z_back = (my_start + (q % wrows) // rows == j).astype(jnp.float32)
    g_ref[0] = big_y * dot(dot(pick_z, vertical), pick_z_back)
    g_ref[1] = dot(g_ref[0], g_ref[0])
    tile = (iota((nx // TILE, nx), 1) // TILE == iota((nx // TILE, nx), 0)).astype(jnp.float32)
    tiles = nx // TILE
    flags = jnp.where(
        iota((tiles, tiles), 0) == iota((tiles, tiles), 1), sea_ref[...].astype(jnp.float32), 0.0
    )
    sea = jnp.sum(jnp.sum(flags, axis=1, keepdims=True) * tile, axis=0, keepdims=True)
    g_parts, a_parts = parts(g_ref[1]), parts(a_ref[1])
    for i in range(2):
        split[0, i, :all_rows, :all_rows] = g_parts[i]
        split[1, i, :nx, :nx] = a_parts[i]

    def gathered(ref, where):
        return jnp.concatenate(
            [ref[where(half)].reshape(all_rows, LANES) for half in range(halves)], axis=1
        )

    own_copies[1].wait()
    own_copies[2].wait()

    @pl.loop(1, n_tm)
    def wait_p(offset):
        index = (here + n_tm - offset) % n_tm
        pltpu.make_async_copy(qbuf.at[index], qbuf.at[index], p_recv.at[index]).wait()

    @pl.loop(1, n_sp)
    def wait_f(offset):
        index = (spot + n_sp - offset) % n_sp
        pltpu.make_async_copy(dbuf.at[index], dbuf.at[index], f_recv.at[index]).wait()

    source[1] = gathered(dbuf, lambda half: (slice(None), 1, half)) * sea
    source[0] = dot(dot(g_ref[0], source[1]), a_ref[0])

    @pl.loop(0, n_tm)
    def make_factors(n):
        log_damp = jnp.log(gathered(dbuf, lambda half: (slice(None), 0, half)))
        phase = qbuf[n]
        weight = 1.0 + 0.5 * jnp.cos(2.0 * math.pi * phase / PHASES)
        first = jnp.cos(2.0 * math.pi * (phase * STEPS) / (PHASES * STEPS))
        second = jnp.cos(2.0 * math.pi * (phase * STEPS + 1) / (PHASES * STEPS))

        def wide(values):
            return jnp.concatenate([values[:1]] * halves, axis=1)

        factor[n] = jnp.exp(wide(weight) * log_damp)
        offset_ref[n] = wide(first) * source[0] + wide(second) * source[1]

    product = factor[0]
    for n in range(1, n_tm):
        product = factor[n] * product
    inverse_p[...] = 1.0 / (1.0 - product)

    def fine(n, field):
        g_split = split[0, 0, :all_rows, :all_rows], split[0, 1, :all_rows, :all_rows]
        a_split = split[1, 0, :nx, :nx], split[1, 1, :nx, :nx]
        moved = dot3(parts(dot3(g_split, parts(field))), a_split)
        state[n] = moved + offset_ref[n] - factor[n] * field

    own_copies[0].wait()

    @pl.loop(1, n_tm + 1)
    def fine_first(turned):
        n = (here + n_tm - turned) % n_tm

        @pl.loop(0, n_sp)
        def wait_u(r):
            @pl.when(n * n_sp + r != me)
            def _():
                slot = xbuf.at[n, r]
                pltpu.make_async_copy(slot, slot, u_recv.at[n * n_sp + r]).wait()

        fine(n, gathered(xbuf, lambda half: (n, slice(None), half)))

    def fine_rows(n, block):
        field = state[n]
        g_split = split[0, 0, block, :all_rows], split[0, 1, block, :all_rows]
        a_split = split[1, 0, :nx, :nx], split[1, 1, :nx, :nx]
        moved = dot3(parts(dot3(g_split, parts(field))), a_split)
        ends[n, block, :] = moved + offset_ref[n, block, :] - factor[n, block, :] * state[n, block, :]

    def solve(r, held, keep):
        block = pl.ds(pl.multiple_of(r * wrows, 8), wrows)
        factors = [factor[n, block, :] for n in range(n_tm)]
        offsets = [held[n, block, :] for n in range(n_tm)]
        total = offsets[0]
        for n in range(1, n_tm):
            total = factors[n] * total + offsets[n]
        fresh = total * inverse_p[block, :]
        for n in range(n_tm):
            keep(n, block, fresh)
            fresh = factors[n] * fresh + offsets[n]

    def keep_state(n, block, values):
        state[n, block, :] = values

    for iteration in range(1, ITERS):
        pl.loop(0, n_sp)(lambda r: solve(r, state, keep_state))
        if iteration < ITERS - 1:
            pl.loop(0, n_tm)(lambda n: fine(n, state[n]))

    inner = pl.multiple_of((my_k * chunk - my_start) * rows, 8)
    back = pltpu.make_async_copy(
        obuf.at[here, spot, :, pl.ds(inner, crows), :],
        rbuf.at[my_t, :, chunk_rows(my_k), :],
        o_recv.at[me],
    )

    near_half = spot // (n_sp // 2)

    @pl.loop(1, 3)
    def last_half(turned_half):
        part = (near_half + turned_half) % 2
        block = pl.ds(pl.multiple_of(part * (all_rows // 2), 16), all_rows // 2)
        for n in range(n_tm):
            fine_rows(n, block)

        @pl.loop(1, n_sp // 2 + 1)
        def solve_last(turned):
            r = part * (n_sp // 2) + (spot + turned) % (n_sp // 2)

            def keep_out(n, rows_block, values):
                for half in range(halves):
                    obuf[n, r, half] = values[:, half * LANES : (half + 1) * LANES]

            solve(r, ends, keep_out)
            for n in range(n_tm):

                @pl.when(n * n_sp + r != me)
                def _():
                    send_o(n * n_sp + r).start()

    back.start()
    back.wait()

    for t in range(n_t):

        @pl.loop(t * per, (t + 1) * per)
        def wait_o(index):
            @pl.when(index != me)
            def _():
                slot = rbuf.at[t, :, chunk_rows(index % per), :]
                pltpu.make_async_copy(slot, slot, o_recv.at[index]).wait()

        for half in range(halves):
            for y in range(rows):
                part = rbuf[t, half, pl.ds(y, nz, stride=rows), :]
                out_ref[t, pl.ds(half * LANES * rows + y, LANES, stride=rows), :] = part.T

    @pl.loop(1, count)
    def sent(offset):
        send_u(offset).wait_send()
        send_o((me + offset) % count).wait_send()

    @pl.loop(1, n_sp)
    def sent_f(offset):
        send_f(offset).wait_send()

    @pl.loop(1, n_tm)
    def sent_p(offset):
        send_p(offset).wait_send()


def whole_period(init_states, forcing, damp, kappa_x, kappa_y, kappa_z, sea_tiles, phases):
    n_tm, n_sp = lax.axis_size("tm"), lax.axis_size("space")
    n_t, _, nx, rows, nz = init_states.shape
    count = n_tm * n_sp
    chunk = nz // (count // n_t)
    window = chunk + 2 * HALO
    halves = nx // LANES
    wrows = window * rows
    all_rows = n_sp * wrows
    flat = (n_t, nx * rows, nz)
    vmem = pl.BlockSpec(memory_space=pltpu.VMEM)
    f32 = jnp.float32
    out = pl.pallas_call(
        functools.partial(period_kernel, (n_tm, n_sp, n_t, nx, rows, nz)),
        out_shape=jax.ShapeDtypeStruct(flat, f32),
        in_specs=[pl.BlockSpec(memory_space=pltpu.HBM)] * 7 + [pl.BlockSpec(memory_space=pltpu.SMEM)],
        out_specs=vmem,
        scratch_shapes=[
            pltpu.VMEM(flat, f32),
            pltpu.VMEM(flat, f32),
            pltpu.VMEM(flat, f32),
            pltpu.VMEM((1, nx), f32),
            pltpu.VMEM((1, kappa_y.shape[0]), f32),
            pltpu.VMEM((1, nz), f32),
            pltpu.VMEM((1, sea_tiles.shape[0]), jnp.int32),
            pltpu.SemaphoreType.DMA((7,)),
            pltpu.VMEM((all_rows, nx), f32),
            pltpu.VMEM((2, 2, max(all_rows, nx), max(all_rows, nx)), jnp.bfloat16),
            pltpu.VMEM((n_tm, all_rows, nx), f32),
            pltpu.VMEM((n_t, halves, nz * rows, LANES), f32),
            pltpu.VMEM((n_t, 2, halves, nz * rows, LANES), f32),
            pltpu.VMEM((8, LANES), f32),
            pltpu.VMEM((n_tm, n_sp, halves, wrows, LANES), f32),
            pltpu.VMEM((n_sp, 2, halves, wrows, LANES), f32),
            pltpu.VMEM((n_tm, 8, LANES), f32),
            pltpu.VMEM((n_tm, n_sp, halves, wrows, LANES), f32),
            pltpu.VMEM((n_t, halves, nz * rows, LANES), f32),
            pltpu.VMEM((2, all_rows, all_rows), f32),
            pltpu.VMEM((2, nx, nx), f32),
            pltpu.VMEM((n_tm, all_rows, nx), f32),
            pltpu.VMEM((n_tm, all_rows, nx), f32),
            pltpu.VMEM((2, all_rows, nx), f32),
            pltpu.VMEM((n_tm, all_rows, nx), f32),
            pltpu.SemaphoreType.DMA((count,)),
            pltpu.SemaphoreType.DMA((count,)),
            pltpu.SemaphoreType.DMA((n_sp,)),
            pltpu.SemaphoreType.DMA((n_sp,)),
            pltpu.SemaphoreType.DMA((n_tm,)),
            pltpu.SemaphoreType.DMA((n_tm,)),
            pltpu.SemaphoreType.DMA((count,)),
            pltpu.SemaphoreType.DMA((count,)),
        ],
        compiler_params=pltpu.CompilerParams(
            collective_id=0, has_side_effects=True, vmem_limit_bytes=63 * 1024 * 1024
        ),
    )(
        init_states.reshape(flat),
        forcing.reshape(flat),
        damp.reshape(flat),
        kappa_x[None],
        kappa_y[None],
        kappa_z[None],
        sea_tiles.reshape(1, -1),
        phases,
    )
    return out.reshape(init_states.shape)


def choose(init_states, forcing, damp, kappa_x, kappa_y, kappa_z, sea_tiles, phases):
    count = lax.axis_size("tm") * lax.axis_size("space")
    n_t, slabs, nx, rows, nz = init_states.shape
    ny = lax.axis_size("space") * rows
    per = count // n_t
    fits = (
        slabs == 1
        and count % n_t == 0
        and nz == LANES
        and nx % LANES == 0
        and nz % per == 0
        and (nz // per * rows) % 8 == 0
        and (HALO * rows) % 8 == 0
        and nz // per + 2 * HALO <= nz
        and ny <= LANES
        and ny & (ny - 1) == 0
        and sea_tiles.shape[1] == 1
        and lax.axis_size("space") % 2 == 0
        and lax.axis_size("space") * (nz // per + 2 * HALO) * rows <= 512
    )
    run = whole_period if fits else body
    return run(init_states, forcing, damp, kappa_x, kappa_y, kappa_z, sea_tiles, phases)


def solution(mesh):
    return jax.shard_map(
        choose,
        mesh=mesh,
        in_specs=(
            P(None, "tm", None, "space", None),
            P(None, None, "space", None),
            P(None, None, "space", None),
            P(),
            P(),
            P(),
            P(),
            P("tm"),
        ),
        out_specs=P(None, "tm", None, "space", None),
        check_vma=False,
    )
```

profile of v0, /device:TPU:0, one launch (start us, length us, event | category | flops | bytes accessed | tf_op | source)
XLA Modules:
  0.0 62.0 jit_solution(17281524028517046686)
XLA Ops:
  0.7 59.5 %shard_map.82 = f32[2,512,128]{2,1,0:T(8,128)} custom-call(f32[2,512,128]{2,1,0:T(8,128)} %bitcast.11, f32[2,512,128]{2,1,0:T(8,128)} %bitcast.12, f32[2,512,128]{2,1,0:T(8,128)} %bitcast.13, f32[1,256]{1,0:T(1,128)} %bitcast.14, f32[1,16]{1,0:T(1,128)} %bitcast.15, f32[1,128]{1,0:T(1,128)} %bitcast.16, s32[1,16]{1,0:T(1,128)} %bitcast.17, s32[1]{0:T(128)S(6)} %copy.11.phase_ref), custom_call_target="tpu_custom_call" | custom-call | tf_op jit(solution)/shard_map/pallas_call | solution.py:521
  60.1 1.9 %copy.12 = f32[2,1,256,2,128]{4,3,2,1,0:T(2,128)} copy(f32[2,1,256,2,128]{4,3,2,1,0:T(2,128)} %bitcast.10) | data formatting | bytes 1048576
where the time goes:
time: 62.2 us; the launch traced here: 62 us
  Pallas kernels  59.5 us (96%)
  local copies, waits for them, and re-layouts  1.87 us (3%)
  between operations  0.66 us (1%)
    pallas_call x1, Pallas kernels, whole_period(): pl.pallas_call(functools.partial(period_kernel, (n_tm, n_sp, n_t, nx, row...  59.5 us
    unnamed x1, local copies, waits for them, and re-layouts  1.87 us

commit v1 on v0

v1 whole, which is shorter than its diff:
```python
import functools
import math

import jax
import jax.numpy as jnp
from jax import lax
from jax.experimental import pallas as pl
from jax.experimental.pallas import tpu as pltpu
from jax.sharding import PartitionSpec as P

STEPS = 2
ITERS = 2
TILE = 16
PHASES = 12


def shifted(array, axis, by):
    devices = lax.axis_size(axis)
    return lax.ppermute(array, axis, [(i, (i + by) % devices) for i in range(devices)])


def line_inverse(kappa):
    face = 0.5 * (kappa[1:] + kappa[:-1])
    zero = jnp.zeros((1,), kappa.dtype)
    left = jnp.concatenate([zero, face])
    right = jnp.concatenate([face, zero])
    identity = jnp.eye(kappa.shape[0], dtype=kappa.dtype)
    return lax.linalg.tridiagonal_solve(-left, 1.0 + left + right, -right, identity)


def solve_lines(field, inverse):
    return jnp.matmul(inverse, field, precision=lax.Precision.HIGHEST)


def solve_x(field, inverse):
    shape = field.shape
    flat = field.reshape(shape[0], shape[1], shape[2], shape[3] * shape[4])
    return solve_lines(flat, inverse).reshape(shape)


def vertical_mix(field, kappa_z):
    face = 0.5 * (kappa_z[1:] + kappa_z[:-1])
    flux = face * (field[..., 1:] - field[..., :-1])
    zeros = jnp.zeros(field.shape[:-1] + (1,), field.dtype)
    flux = jnp.concatenate([zeros, flux, zeros], axis=-1)
    return field + flux[..., 1:] - flux[..., :-1]


def compose(earlier, later):
    return (earlier[0] * later[0], later[0] * earlier[1] + later[1])


def column_pass(field, inverse_y):
    return lax.all_to_all(
        solve_lines(
            lax.all_to_all(field, "space", split_axis=2, concat_axis=3, tiled=True), inverse_y
        ),
        "space",
        split_axis=3,
        concat_axis=2,
        tiled=True,
    )


def body(init_states, forcing, damp, kappa_x, kappa_y, kappa_z, sea_tiles, phases):
    row_count = init_states.shape[3]
    inverse_x = line_inverse(kappa_x)
    inverse_y = line_inverse(kappa_y)
    tiles = sea_tiles.astype(jnp.float32)
    sea = jnp.repeat(jnp.repeat(tiles, TILE, axis=0), TILE, axis=1)
    sea_rows = lax.dynamic_slice_in_dim(sea, lax.axis_index("space") * row_count, row_count, 1)
    source = (forcing * sea_rows[None, :, :, None])[:, None]
    phase_float = phases.astype(jnp.float32)
    weight = 1.0 + 0.5 * jnp.cos(2.0 * math.pi * phase_float / PHASES)
    factors = jnp.exp(weight[None, :, None, None, None] * jnp.log(damp)[:, None])
    states = init_states
    for iteration in range(ITERS):
        field = states
        for step in range(STEPS):
            amplitude = jnp.cos(2.0 * math.pi * (phase_float * STEPS + step) / (PHASES * STEPS))[
                None, :, None, None, None
            ]
            if step % 2 == 0:
                field = column_pass(solve_x(field, inverse_x), inverse_y)
            else:
                field = solve_x(column_pass(field, inverse_y), inverse_x)
            field = vertical_mix(field, kappa_z) + amplitude * source
        offsets = field - factors * states
        own_factor = factors[:, 0]
        own_offset = offsets[:, 0]
        own = (own_factor, own_offset)
        ident = (jnp.ones_like(own_factor), jnp.zeros_like(own_offset))
        count = lax.axis_size("tm")
        here = lax.axis_index("tm")
        lower_part = ident
        upper_part = ident
        moving = jnp.stack([own_factor, own_offset])
        for turn in range(1, count):
            moving = shifted(moving, "tm", 1)
            piece = (moving[0], moving[1])
            anchor = (here - turn) % count
            before = anchor < here
            joined_low = compose(piece, lower_part)
            joined_high = compose(piece, upper_part)
            lower_part = (
                jnp.where(before, joined_low[0], lower_part[0]),
                jnp.where(before, joined_low[1], lower_part[1]),
            )
            upper_part = (
                jnp.where(before, upper_part[0], joined_high[0]),
                jnp.where(before, upper_part[1], joined_high[1]),
            )
        period = compose(compose(lower_part, own), upper_part)
        first = period[1] / (1.0 - period[0])
        start = lower_part[0] * first + lower_part[1]
        fresh = [start]
        states = jnp.stack(fresh, axis=1)
    return states


LANES = 128
HALO = 2 * ITERS
MESH = pl.DeviceIdType.MESH


def dot(a, b):
    return jnp.dot(a, b, precision=lax.Precision.HIGHEST, preferred_element_type=jnp.float32)


def parts(a):
    high = a.astype(jnp.bfloat16)
    return high, (a - high.astype(jnp.float32)).astype(jnp.bfloat16)


def dot3(a, b):
    once = functools.partial(jnp.dot, preferred_element_type=jnp.float32)
    return once(a[0], b[0]) + (once(a[0], b[1]) + once(a[1], b[0]))


def iota(shape, axis):
    return lax.broadcasted_iota(jnp.int32, shape, axis)


def faces(kappa_row, n):
    row, col = iota((n, n), 0), iota((n, n), 1)
    own = jnp.sum(jnp.where(row == col, kappa_row, 0.0), axis=1, keepdims=True)
    face = 0.5 * (own + kappa_row)
    below = jnp.where(col == row - 1, face, 0.0)
    above = jnp.where(col == row + 1, face, 0.0)
    return (
        jnp.sum(below, axis=1, keepdims=True),
        jnp.sum(above, axis=1, keepdims=True),
        below + above,
    )


def reduced_inverse(kappa_row, n):
    lower, upper, _ = faces(kappa_row, n)
    shape = (n, LANES)
    a = jnp.broadcast_to(-lower, shape)
    c = jnp.broadcast_to(-upper, shape)
    b = 1.0 - a - c
    blocks = [
        (iota(shape, 0) == iota(shape, 1) + LANES * j).astype(jnp.float32)
        for j in range(max(n // LANES, 1))
    ]
    s = 1
    while s < n:
        before = functools.partial(pltpu.roll, shift=s, axis=0)
        after = functools.partial(pltpu.roll, shift=n - s, axis=0)
        alpha = -a / before(b)
        gamma = -c / after(b)
        blocks = [d + alpha * before(d) + gamma * after(d) for d in blocks]
        b = b + alpha * before(c) + gamma * after(a)
        a, c = alpha * before(a), gamma * after(c)
        s *= 2
    inverse = 1.0 / b
    return [d * inverse for d in blocks]


def copied(pick, a):
    high, low = parts(a)
    once = functools.partial(jnp.dot, preferred_element_type=jnp.float32)
    return once(pick, high) + once(pick, low)


def spread(a, pick):
    high, low = parts(a)
    once = functools.partial(jnp.dot, preferred_element_type=jnp.float32)
    return once(high, pick) + once(low, pick)


def period_kernel(
    size, u_hbm, f_hbm, damp_hbm, kx_hbm, ky_hbm, kz_hbm, sea_hbm, phase_ref, out_ref,
    u_ref, f_ref, damp_ref, kx_ref, ky_ref, kz_ref, sea_ref, fetched, inverse_p,
    g_split, a_split, g_ref, a_ref, w_high, w_low, ends,
    ubuf, fbuf, pbuf, xbuf, dbuf, qbuf, obuf, rbuf, state, factor, source, offset_ref,
    near_out, near_in, last_out, last_in,
    u_send, u_recv, f_send, f_recv, p_send, p_recv, o_send, o_recv,
    near_send, near_recv, last_send, last_recv,
):
    n_tm, n_sp, n_t, nx, rows, nz = size
    spots = n_sp // 2
    count = n_tm * spots
    per = count // n_t
    chunk = nz // per
    window = chunk + 2 * HALO
    halves = nx // LANES
    wrows = window * rows
    crows = chunk * rows
    all_rows = spots * wrows
    tail, kept = 2 * chunk, 2 * (chunk + HALO)
    ext = LANES * -(-(all_rows + kept) // LANES)
    ny = n_sp * rows

    here = lax.axis_index("tm")
    space = lax.axis_index("space")
    side, spot = space // spots, space % spots
    me = here * spots + spot
    across = {"tm": here, "space": (1 - side) * spots + spot}

    def window_start(k):
        return jnp.minimum(jnp.maximum(k * chunk - HALO, 0), nz - window)

    def window_rows(k):
        return pl.ds(pl.multiple_of(window_start(k) * rows, 8), wrows)

    def chunk_rows(k):
        return pl.ds(pl.multiple_of(k * crows, 8), crows)

    def device(index):
        return {"tm": index // spots, "space": side * spots + index % spots}

    pairs = (
        (u_hbm, u_ref),
        (f_hbm, f_ref),
        (damp_hbm, damp_ref),
        (kx_hbm, kx_ref),
        (ky_hbm, ky_ref),
        (kz_hbm, kz_ref),
        (sea_hbm, sea_ref),
    )
    fetches = [
        pltpu.make_async_copy(far, near, fetched.at[i]) for i, (far, near) in enumerate(pairs)
    ]
    for fetch in fetches:
        fetch.start()

    barrier = pltpu.get_barrier_semaphore()

    @pl.loop(1, count)
    def greet(offset):
        pl.semaphore_signal(
            barrier, inc=1, device_id=device((me + offset) % count), device_id_type=MESH
        )

    pl.semaphore_signal(barrier, inc=1, device_id=across, device_id_type=MESH)

    def turn(ref, buf, where):
        for t in range(n_t):
            for half in range(halves):
                for y in range(rows):
                    part = ref[t, pl.ds(half * LANES * rows + y, LANES, stride=rows), :]
                    buf[(t, *where, half, pl.ds(y, nz, stride=rows), slice(None))] = part.T

    pbuf[...] = jnp.full((8, LANES), phase_ref[0].astype(jnp.float32))

    my_t, my_k = me // per, me % per
    my_start = window_start(my_k)

    own_u = pltpu.make_async_copy(
        ubuf.at[my_t, :, window_rows(my_k), :], xbuf.at[here, spot], u_recv.at[me]
    )
    own_f = [
        pltpu.make_async_copy(
            fbuf.at[my_t, which, :, window_rows(my_k), :],
            dbuf.at[which, spot],
            f_recv.at[which, spot],
        )
        for which in range(2)
    ]
    own_p = pltpu.make_async_copy(pbuf, qbuf.at[here], p_recv.at[here])

    def send_u(offset):
        index = (me + offset) % count
        return pltpu.make_async_remote_copy(
            src_ref=ubuf.at[index // per, :, window_rows(index % per), :],
            dst_ref=xbuf.at[here, spot],
            send_sem=u_send.at[offset],
            recv_sem=u_recv.at[me],
            device_id=device(index),
            device_id_type=MESH,
        )

    def send_f(which, offset):
        index = here * spots + (spot + offset) % spots
        return pltpu.make_async_remote_copy(
            src_ref=fbuf.at[index // per, which, :, window_rows(index % per), :],
            dst_ref=dbuf.at[which, spot],
            send_sem=f_send.at[which, offset],
            recv_sem=f_recv.at[which, spot],
            device_id=device(index),
            device_id_type=MESH,
        )

    def send_p(offset):
        return pltpu.make_async_remote_copy(
            src_ref=pbuf,
            dst_ref=qbuf.at[here],
            send_sem=p_send.at[offset],
            recv_sem=p_recv.at[here],
            device_id={"tm": (here + offset) % n_tm, "space": space},
            device_id_type=MESH,
        )

    def send_near(n):
        return pltpu.make_async_remote_copy(
            src_ref=near_out.at[n],
            dst_ref=near_in.at[n],
            send_sem=near_send.at[n],
            recv_sem=near_recv.at[n],
            device_id=across,
            device_id_type=MESH,
        )

    def send_last(n, half):
        return pltpu.make_async_remote_copy(
            src_ref=last_out.at[n, half],
            dst_ref=last_in.at[n, half],
            send_sem=last_send.at[n, half],
            recv_sem=last_recv.at[n, half],
            device_id=across,
            device_id_type=MESH,
        )

    def send_o(half, index):
        return pltpu.make_async_remote_copy(
            src_ref=obuf.at[half, index // spots, index % spots],
            dst_ref=rbuf.at[half, my_t, chunk_rows(my_k), :],
            send_sem=o_send.at[half, index],
            recv_sem=o_recv.at[half, me],
            device_id=device(index),
            device_id_type=MESH,
        )

    fetches[0].wait()
    turn(u_ref, ubuf, ())
    pl.semaphore_wait(barrier, count)

    @pl.loop(1, n_tm)
    def start_p(offset):
        send_p(offset).start()

    @pl.loop(1, count // 2 + 1)
    def start_u(offset):
        send_u(offset).start()

    own_p.start()
    own_u.start()
    fetches[1].wait()
    turn(f_ref, fbuf, (0,))

    @pl.loop(1, spots)
    def start_f(offset):
        send_f(0, offset).start()

    own_f[0].start()

    @pl.loop(count // 2 + 1, count)
    def start_u_rest(offset):
        send_u(offset).start()

    fetches[2].wait()
    turn(damp_ref, fbuf, (1,))

    @pl.loop(1, spots)
    def start_damp(offset):
        send_f(1, offset).start()

    own_f[1].start()
    for fetch in fetches[3:]:
        fetch.wait()

    for half, block in enumerate(reduced_inverse(kx_ref[...], nx)):
        a_ref[:, half * LANES : (half + 1) * LANES] = block
    a_once = a_ref[...]
    for i, part in enumerate(parts(a_once)):
        a_split[0, i] = part
    for i, part in enumerate(parts(dot(a_once, a_once))):
        a_split[1, i] = part

    inverse_y = reduced_inverse(ky_ref[...], ny)[0]
    row, col = iota((ny, LANES), 0), iota((ny, LANES), 1)
    edge, far_edge = ny // 2 - 1 + side, ny // 2 - side
    own_row, own_col = row // (ny // 2) == side, col // (ny // 2) == side
    inner_y = jnp.where(own_row & own_col, inverse_y, 0.0)
    twice_y = dot(inverse_y[:, :ny], inverse_y)
    inner_twice = dot(inner_y[:, :ny], inner_y)
    corner = jnp.sum(
        jnp.sum(
            jnp.where((row == far_edge) & (col == far_edge), inverse_y, 0.0), axis=1, keepdims=True
        ),
        axis=0,
        keepdims=True,
    )
    leave_once = jnp.sum(jnp.where(row == edge, inner_y, 0.0), axis=0, keepdims=True)
    leave_twice = jnp.sum(jnp.where(row == edge, inner_twice, 0.0), axis=0, keepdims=True)
    enter_line = (
        jnp.sum(jnp.where((row == far_edge) & own_col, inverse_y, 0.0), axis=0, keepdims=True)
        / corner
    )
    enter_once = (
        jnp.sum(jnp.where((col == far_edge) & own_row, inverse_y, 0.0), axis=1, keepdims=True)
        / corner
    )
    enter_twice = jnp.sum(inner_y * enter_line, axis=1, keepdims=True)
    below = iota((ny, LANES), 0)
    ext_y_once = jnp.concatenate(
        [
            inverse_y + jnp.where(col == ny, enter_once, 0.0),
            jnp.where(below == 0, leave_once, 0.0),
        ],
        axis=0,
    )
    ext_y_twice = jnp.concatenate(
        [
            twice_y
            + jnp.where(col == ny, enter_twice, 0.0)
            + jnp.where(col == ny + 1, enter_once, 0.0),
            jnp.where(below == 0, leave_once, jnp.where(below == 1, leave_twice, 0.0)),
        ],
        axis=0,
    )

    def line_of(q):
        own = side * (ny // 2) + (q // wrows) * rows + q % rows
        return jnp.where(q < all_rows, own, ny + q % 2)

    def level_of(q):
        own = my_start + (q % wrows) // rows
        p = (q - all_rows) // 2
        first = my_k * chunk
        ring = jnp.where(p < chunk + HALO // 2, first - HALO // 2 - chunk, first - HALO // 2) + p
        passed = jnp.where(p < chunk, first + p, ring)
        return jnp.where(q < all_rows, own, jnp.where(q < all_rows + kept, passed, -1))

    def mask(a, b):
        return jnp.where(a == b, 1.0, 0.0).astype(jnp.bfloat16)

    pick_y = mask(line_of(iota((ext, 2 * ny), 0)), iota((ext, 2 * ny), 1))
    pick_y_back = mask(line_of(iota((LANES, ext), 1)), iota((LANES, ext), 0))
    pick_z = mask(level_of(iota((ext, nz), 0)), iota((ext, nz), 1))
    pick_z_back = mask(level_of(iota((nz, ext), 1)), iota((nz, ext), 0))
    own_columns = iota((nz, ext), 1) < all_rows
    _, _, beside = faces(kz_ref[...], nz)
    identity = (iota((nz, nz), 0) == iota((nz, nz), 1)).astype(jnp.float32)
    vertical = beside + identity * (1.0 - jnp.sum(beside, axis=1, keepdims=True))
    for order, (ext_y, mixed) in enumerate(
        ((ext_y_once, vertical), (ext_y_twice, dot(vertical, vertical)))
    ):
        across_y = spread(copied(pick_y, ext_y), pick_y_back)
        levels = jnp.where(own_columns, spread(mixed, pick_z_back), pick_z_back.astype(jnp.float32))
        whole = across_y * copied(pick_z, levels)
        for i, part in enumerate(parts(whole)):
            g_split[order, i] = part
    g_ref[...] = whole
    inner = (my_k * chunk - my_start) * rows

    def inner_rows(r):
        return pl.ds(pl.multiple_of(r * wrows + inner, 8), crows)

    for i, part in enumerate(
        parts(jnp.concatenate([g_ref[inner_rows(r), :] for r in range(spots)], axis=0))
    ):
        g_split[2, i, : spots * crows, :] = part

    w_high[:, all_rows:, :] = jnp.zeros((n_tm + 1, ext - all_rows, nx), jnp.bfloat16)
    w_low[:, all_rows:, :] = jnp.zeros((n_tm + 1, ext - all_rows, nx), jnp.bfloat16)

    tile = (iota((nx // TILE, nx), 1) // TILE == iota((nx // TILE, nx), 0)).astype(jnp.float32)
    tiles = nx // TILE
    flags = jnp.where(
        iota((tiles, tiles), 0) == iota((tiles, tiles), 1), sea_ref[...].astype(jnp.float32), 0.0
    )
    sea = jnp.sum(jnp.sum(flags, axis=1, keepdims=True) * tile, axis=0, keepdims=True)

    def gathered(ref, where):
        return jnp.concatenate(
            [ref[where(half)].reshape(all_rows, LANES) for half in range(halves)], axis=1
        )

    def solve_x_lines(n, order, field):
        moved = dot3(parts(field), (a_split[order, 0], a_split[order, 1]))
        w_high[n, :all_rows, :], w_low[n, :all_rows, :] = parts(moved)

    def leaving(n, order, lines):
        padded = 16 * -(-lines // 16)
        block = slice(all_rows, all_rows + padded)
        found = dot3(
            (g_split[order, 0, block, :], g_split[order, 1, block, :]), (w_high[n], w_low[n])
        )
        return found[:lines]

    def joined(n, order):
        w_high[n, all_rows:, :], w_low[n, all_rows:, :] = parts(
            jnp.concatenate(
                [near_in[n], jnp.zeros((ext - all_rows - kept, nx), jnp.float32)], axis=0
            )
        )
        block = slice(0, all_rows)
        return dot3(
            (g_split[order, 0, block, :], g_split[order, 1, block, :]), (w_high[n], w_low[n])
        )

    def arrive_u(turned):
        n = (here + n_tm - turned) % n_tm

        @pl.loop(0, spots)
        def wait_u(r):
            slot = xbuf.at[n, r]
            pltpu.make_async_copy(slot, slot, u_recv.at[n * spots + r]).wait()

        solve_x_lines(n, 1, gathered(xbuf, lambda half: (n, slice(None), half)))
        near_out[n] = leaving(n, 1, kept)
        send_near(n).start()

    pl.loop(1, n_tm // 2 + 1)(arrive_u)

    @pl.loop(0, spots)
    def wait_f(r):
        slot = dbuf.at[0, r]
        pltpu.make_async_copy(slot, slot, f_recv.at[0, r]).wait()

    source[1] = gathered(dbuf, lambda half: (0, slice(None), half)) * sea
    solve_x_lines(n_tm, 0, source[1])
    near_out[n_tm] = leaving(n_tm, 0, kept)
    send_near(n_tm).start()

    pl.loop(n_tm // 2 + 1, n_tm + 1)(arrive_u)

    @pl.loop(0, n_tm)
    def wait_p(n):
        pltpu.make_async_copy(qbuf.at[n], qbuf.at[n], p_recv.at[n]).wait()

    @pl.loop(0, spots)
    def wait_damp(r):
        slot = dbuf.at[1, r]
        pltpu.make_async_copy(slot, slot, f_recv.at[1, r]).wait()

    def wide(values):
        return jnp.concatenate([values[:1]] * halves, axis=1)

    log_damp = jnp.log(gathered(dbuf, lambda half: (1, slice(None), half)))
    product = None
    for n in range(n_tm):
        weight = 1.0 + 0.5 * jnp.cos(2.0 * math.pi * qbuf[n] / PHASES)
        one = jnp.exp(wide(weight) * log_damp)
        factor[n] = one
        product = one if product is None else one * product
    inverse_p[...] = 1.0 / (1.0 - product)

    def wait_near(n):
        pltpu.make_async_copy(near_in.at[n], near_in.at[n], near_recv.at[n]).wait()

    wait_near(n_tm)
    source[0] = joined(n_tm, 0)

    @pl.loop(0, n_tm)
    def make_offsets(n):
        phase = qbuf[n]
        first = jnp.cos(2.0 * math.pi * (phase * STEPS) / (PHASES * STEPS))
        second = jnp.cos(2.0 * math.pi * (phase * STEPS + 1) / (PHASES * STEPS))
        offset_ref[n] = wide(first) * source[0] + wide(second) * source[1]

    @pl.loop(1, n_tm + 1)
    def finish_first(turned):
        n = (here + n_tm - turned) % n_tm
        wait_near(n)
        field = gathered(xbuf, lambda half: (n, slice(None), half))
        state[n] = joined(n, 1) + offset_ref[n] - factor[n] * field

    @pl.loop(0, spots)
    def solve_first(r):
        block = pl.ds(pl.multiple_of(r * wrows, 8), wrows)
        factors = [factor[n, block, :] for n in range(n_tm)]
        offsets = [state[n, block, :] for n in range(n_tm)]
        total = offsets[0]
        for n in range(1, n_tm):
            total = factors[n] * total + offsets[n]
        fresh = total * inverse_p[block, :]
        for n in range(n_tm):
            state[n, block, :] = fresh
            fresh = factors[n] * fresh + offsets[n]

    def lanes(half):
        return slice(half * LANES, (half + 1) * LANES)

    @pl.loop(0, n_tm)
    def leave_last(n):
        solve_x_lines(n, 1, state[n])
        found = leaving(n, 1, tail)
        for half in range(halves):
            last_out[n, half] = found[:, lanes(half)]
        send_last(n, 0).start()

    for half in range(1, halves):

        @pl.loop(0, n_tm)
        def start_last(n):
            send_last(n, half).start()

    for half in range(halves):

        @pl.loop(0, n_tm)
        def finish_last(n):
            slot = last_in.at[n, half]
            pltpu.make_async_copy(slot, slot, last_recv.at[n, half]).wait()
            block = slice(all_rows, all_rows + tail)
            high, low = parts(last_in[n, half])
            w_high[n, block, lanes(half)] = high
            w_low[n, block, lanes(half)] = low
            upper = slice(0, spots * crows)
            ends[n] = dot3(
                (g_split[2, 0, upper, :], g_split[2, 1, upper, :]),
                (w_high[n, :, lanes(half)], w_low[n, :, lanes(half)]),
            )

        @pl.loop(1, spots + 1)
        def solve_last(turned):
            r = (spot + turned) % spots
            block = inner_rows(r)
            packed = pl.ds(pl.multiple_of(r * crows, 8), crows)
            factors = [factor[n, block, lanes(half)] for n in range(n_tm)]
            offsets = [
                ends[n, packed, :]
                + offset_ref[n, block, lanes(half)]
                - factors[n] * state[n, block, lanes(half)]
                for n in range(n_tm)
            ]
            total = offsets[0]
            for n in range(1, n_tm):
                total = factors[n] * total + offsets[n]
            fresh = total * inverse_p[block, lanes(half)]
            for n in range(n_tm):
                obuf[half, n, r] = fresh
                fresh = factors[n] * fresh + offsets[n]
            for n in range(n_tm):

                @pl.when(n * spots + r != me)
                def _():
                    send_o(half, n * spots + r).start()

        pltpu.make_async_copy(
            obuf.at[half, here, spot], rbuf.at[half, my_t, chunk_rows(my_k), :], o_recv.at[half, me]
        ).start()

    for half in range(halves):
        for t in range(n_t):

            @pl.loop(t * per, (t + 1) * per)
            def wait_o(index):
                slot = rbuf.at[half, t, chunk_rows(index % per), :]
                pltpu.make_async_copy(slot, slot, o_recv.at[half, index]).wait()

            for y in range(rows):
                part = rbuf[half, t, pl.ds(y, nz, stride=rows), :]
                out_ref[t, pl.ds(half * LANES * rows + y, LANES, stride=rows), :] = part.T

    @pl.loop(1, count)
    def sent(offset):
        send_u(offset).wait_send()
        for half in range(halves):
            send_o(half, (me + offset) % count).wait_send()

    @pl.loop(1, spots)
    def sent_f(offset):
        for which in range(2):
            send_f(which, offset).wait_send()

    @pl.loop(1, n_tm)
    def sent_p(offset):
        send_p(offset).wait_send()

    @pl.loop(0, n_tm + 1)
    def sent_near(n):
        send_near(n).wait_send()

    @pl.loop(0, n_tm)
    def sent_last(n):
        for half in range(halves):
            send_last(n, half).wait_send()


def whole_period(init_states, forcing, damp, kappa_x, kappa_y, kappa_z, sea_tiles, phases):
    n_tm, n_sp = lax.axis_size("tm"), lax.axis_size("space")
    n_t, _, nx, rows, nz = init_states.shape
    spots = n_sp // 2
    count = n_tm * spots
    chunk = nz // (count // n_t)
    window = chunk + 2 * HALO
    halves = nx // LANES
    wrows = window * rows
    crows = chunk * rows
    all_rows = spots * wrows
    tail, kept = 2 * chunk, 2 * (chunk + HALO)
    ext = LANES * -(-(all_rows + kept) // LANES)
    flat = (n_t, nx * rows, nz)
    vmem = pl.BlockSpec(memory_space=pltpu.VMEM)
    f32 = jnp.float32
    bf16 = jnp.bfloat16
    out = pl.pallas_call(
        functools.partial(period_kernel, (n_tm, n_sp, n_t, nx, rows, nz)),
        out_shape=jax.ShapeDtypeStruct(flat, f32),
        in_specs=[pl.BlockSpec(memory_space=pltpu.HBM)] * 7 + [pl.BlockSpec(memory_space=pltpu.SMEM)],
        out_specs=vmem,
        scratch_shapes=[
            pltpu.VMEM(flat, f32),
            pltpu.VMEM(flat, f32),
            pltpu.VMEM(flat, f32),
            pltpu.VMEM((1, nx), f32),
            pltpu.VMEM((1, kappa_y.shape[0]), f32),
            pltpu.VMEM((1, nz), f32),
            pltpu.VMEM((1, sea_tiles.shape[0]), jnp.int32),
            pltpu.SemaphoreType.DMA((7,)),
            pltpu.VMEM((all_rows, nx), f32),
            pltpu.VMEM((3, 2, ext, ext), bf16),
            pltpu.VMEM((2, 2, nx, nx), bf16),
            pltpu.VMEM((ext, ext), f32),
            pltpu.VMEM((nx, nx), f32),
            pltpu.VMEM((n_tm + 1, ext, nx), bf16),
            pltpu.VMEM((n_tm + 1, ext, nx), bf16),
            pltpu.VMEM((n_tm, spots * crows, LANES), f32),
            pltpu.VMEM((n_t, halves, nz * rows, LANES), f32),
            pltpu.VMEM((n_t, 2, halves, nz * rows, LANES), f32),
            pltpu.VMEM((8, LANES), f32),
            pltpu.VMEM((n_tm, spots, halves, wrows, LANES), f32),
            pltpu.VMEM((2, spots, halves, wrows, LANES), f32),
            pltpu.VMEM((n_tm, 8, LANES), f32),
            pltpu.VMEM((halves, n_tm, spots, crows, LANES), f32),
            pltpu.VMEM((halves, n_t, nz * rows, LANES), f32),
            pltpu.VMEM((n_tm, all_rows, nx), f32),
            pltpu.VMEM((n_tm, all_rows, nx), f32),
            pltpu.VMEM((2, all_rows, nx), f32),
            pltpu.VMEM((n_tm, all_rows, nx), f32),
            pltpu.VMEM((n_tm + 1, kept, nx), f32),
            pltpu.VMEM((n_tm + 1, kept, nx), f32),
            pltpu.VMEM((n_tm, halves, tail, LANES), f32),
            pltpu.VMEM((n_tm, halves, tail, LANES), f32),
            pltpu.SemaphoreType.DMA((count,)),
            pltpu.SemaphoreType.DMA((count,)),
            pltpu.SemaphoreType.DMA((2, spots)),
            pltpu.SemaphoreType.DMA((2, spots)),
            pltpu.SemaphoreType.DMA((n_tm,)),
            pltpu.SemaphoreType.DMA((n_tm,)),
            pltpu.SemaphoreType.DMA((halves, count)),
            pltpu.SemaphoreType.DMA((halves, count)),
            pltpu.SemaphoreType.DMA((n_tm + 1,)),
            pltpu.SemaphoreType.DMA((n_tm + 1,)),
            pltpu.SemaphoreType.DMA((n_tm, halves)),
            pltpu.SemaphoreType.DMA((n_tm, halves)),
        ],
        compiler_params=pltpu.CompilerParams(
            collective_id=0, has_side_effects=True, vmem_limit_bytes=63 * 1024 * 1024
        ),
    )(
        init_states.reshape(flat),
        forcing.reshape(flat),
        damp.reshape(flat),
        kappa_x[None],
        kappa_y[None],
        kappa_z[None],
        sea_tiles.reshape(1, -1),
        phases,
    )
    return out.reshape(init_states.shape)


def choose(init_states, forcing, damp, kappa_x, kappa_y, kappa_z, sea_tiles, phases):
    spots = lax.axis_size("space") // 2
    count = lax.axis_size("tm") * spots
    n_t, slabs, nx, rows, nz = init_states.shape
    ny = lax.axis_size("space") * rows
    per = max(count // n_t, 1)
    chunk = nz // per
    all_rows = spots * (chunk + 2 * HALO) * rows
    fits = (
        ITERS == 2
        and slabs == 1
        and lax.axis_size("space") % 2 == 0
        and lax.axis_size("tm") % 2 == 0
        and count % n_t == 0
        and nz == LANES
        and nx % LANES == 0
        and nz % per == 0
        and chunk * rows % 8 == 0
        and HALO * rows % 8 == 0
        and HALO <= chunk
        and chunk % 8 == 0
        and all_rows % 16 == 0
        and chunk + 2 * HALO <= nz
        and ny + 2 <= LANES
        and ny & (ny - 1) == 0
        and ny >= 16
        and sea_tiles.shape[1] == 1
        and all_rows + 2 * (chunk + HALO) <= 512
    )
    run = whole_period if fits else body
    return run(init_states, forcing, damp, kappa_x, kappa_y, kappa_z, sea_tiles, phases)


def solution(mesh):
    return jax.shard_map(
        choose,
        mesh=mesh,
        in_specs=(
            P(None, "tm", None, "space", None),
            P(None, None, "space", None),
            P(None, None, "space", None),
            P(),
            P(),
            P(),
            P(),
            P("tm"),
        ),
        out_specs=P(None, "tm", None, "space", None),
        check_vma=False,
    )
```

time: 62.2 us -> 44.5 us (0.72)
  Pallas kernels: 59.5 us -> 41.7 us
    pallas_call x1, Pallas kernels: 59.5 us -> 41.7 us  [whole_period(): pl.pallas_call(functools.partial(period_kernel, (n_tm, n_sp, n_t, nx, row...]
where the time goes in v1:
time: 44.5 us; the launch traced here: 44.3 us
  Pallas kernels  41.7 us (94%)
  local copies, waits for them, and re-layouts  1.87 us (4%)
  between operations  0.66 us (1%)
    pallas_call x1, Pallas kernels, whole_period(): pl.pallas_call(functools.partial(period_kernel, (n_tm, n_sp, n_t, nx, row...  41.7 us
    unnamed x1, local copies, waits for them, and re-layouts  1.87 us

profile of v1, /device:TPU:0, one launch (start us, length us, event | category | flops | bytes accessed | tf_op | source)
XLA Modules:
  0.0 44.3 jit_solution(14570861873585784789)
XLA Ops:
  0.7 41.7 %shard_map.82 = f32[2,512,128]{2,1,0:T(8,128)} custom-call(f32[2,512,128]{2,1,0:T(8,128)} %bitcast.11, f32[2,512,128]{2,1,0:T(8,128)} %bitcast.12, f32[2,512,128]{2,1,0:T(8,128)} %bitcast.13, f32[1,256]{1,0:T(1,128)} %bitcast.14, f32[1,16]{1,0:T(1,128)} %bitcast.15, f32[1,128]{1,0:T(1,128)} %bitcast.16, s32[1,16]{1,0:T(1,128)} %bitcast.17, s32[1]{0:T(128)S(6)} %copy.11.phase_ref), custom_call_target="tpu_custom_call" | custom-call | tf_op jit(solution)/shard_map/pallas_call | solution.py:711
  42.4 1.9 %copy.12 = f32[2,1,256,2,128]{4,3,2,1,0:T(2,128)} copy(f32[2,1,256,2,128]{4,3,2,1,0:T(2,128)} %bitcast.10) | data formatting | bytes 1048576

commit v2 on v1

--- a/solution.py
+++ b/solution.py
@@ -194,7 +194,7 @@
     size, u_hbm, f_hbm, damp_hbm, kx_hbm, ky_hbm, kz_hbm, sea_hbm, phase_ref, out_ref,
     u_ref, f_ref, damp_ref, kx_ref, ky_ref, kz_ref, sea_ref, fetched, inverse_p,
     g_split, a_split, g_ref, a_ref, w_high, w_low, ends,
-    ubuf, fbuf, pbuf, xbuf, dbuf, qbuf, obuf, rbuf, state, factor, source, offset_ref,
+    ubuf, fbuf, pbuf, xbuf, dbuf, qbuf, obuf, state, factor, source, offset_ref,
     near_out, near_in, last_out, last_in,
     u_send, u_recv, f_send, f_recv, p_send, p_recv, o_send, o_recv,
     near_send, near_recv, last_send, last_recv,
@@ -269,25 +269,25 @@
     my_start = window_start(my_k)
 
     own_u = pltpu.make_async_copy(
-        ubuf.at[my_t, :, window_rows(my_k), :], xbuf.at[here, spot], u_recv.at[me]
+        ubuf.at[my_t, :, window_rows(my_k), :], xbuf.at[me], u_recv.at[here]
     )
     own_f = [
         pltpu.make_async_copy(
             fbuf.at[my_t, which, :, window_rows(my_k), :],
             dbuf.at[which, spot],
-            f_recv.at[which, spot],
+            f_recv.at[which],
         )
         for which in range(2)
     ]
-    own_p = pltpu.make_async_copy(pbuf, qbuf.at[here], p_recv.at[here])
+    own_p = pltpu.make_async_copy(pbuf, qbuf.at[here], p_recv)
 
     def send_u(offset):
         index = (me + offset) % count
         return pltpu.make_async_remote_copy(
             src_ref=ubuf.at[index // per, :, window_rows(index % per), :],
-            dst_ref=xbuf.at[here, spot],
-            send_sem=u_send.at[offset],
-            recv_sem=u_recv.at[me],
+            dst_ref=xbuf.at[here * spots + spot],
+            send_sem=u_send,
+            recv_sem=u_recv.at[here],
             device_id=device(index),
             device_id_type=MESH,
         )
@@ -297,8 +297,8 @@
         return pltpu.make_async_remote_copy(
             src_ref=fbuf.at[index // per, which, :, window_rows(index % per), :],
             dst_ref=dbuf.at[which, spot],
-            send_sem=f_send.at[which, offset],
-            recv_sem=f_recv.at[which, spot],
+            send_sem=f_send,
+            recv_sem=f_recv.at[which],
             device_id=device(index),
             device_id_type=MESH,
         )
@@ -307,8 +307,8 @@
         return pltpu.make_async_remote_copy(
             src_ref=pbuf,
             dst_ref=qbuf.at[here],
-            send_sem=p_send.at[offset],
-            recv_sem=p_recv.at[here],
+            send_sem=p_send,
+            recv_sem=p_recv,
             device_id={"tm": (here + offset) % n_tm, "space": space},
             device_id_type=MESH,
         )
@@ -317,7 +317,7 @@
         return pltpu.make_async_remote_copy(
             src_ref=near_out.at[n],
             dst_ref=near_in.at[n],
-            send_sem=near_send.at[n],
+            send_sem=near_send,
             recv_sem=near_recv.at[n],
             device_id=across,
             device_id_type=MESH,
@@ -327,7 +327,7 @@
         return pltpu.make_async_remote_copy(
             src_ref=last_out.at[n, half],
             dst_ref=last_in.at[n, half],
-            send_sem=last_send.at[n, half],
+            send_sem=last_send,
             recv_sem=last_recv.at[n, half],
             device_id=across,
             device_id_type=MESH,
@@ -335,10 +335,10 @@
 
     def send_o(half, index):
         return pltpu.make_async_remote_copy(
-            src_ref=obuf.at[half, index // spots, index % spots],
-            dst_ref=rbuf.at[half, my_t, chunk_rows(my_k), :],
-            send_sem=o_send.at[half, index],
-            recv_sem=o_recv.at[half, me],
+            src_ref=obuf.at[half * count + index],
+            dst_ref=out_ref.at[my_t, half, chunk_rows(my_k), :],
+            send_sem=o_send,
+            recv_sem=o_recv,
             device_id=device(index),
             device_id_type=MESH,
         )
@@ -373,11 +373,6 @@
     fetches[2].wait()
     turn(damp_ref, fbuf, (1,))
 
-    @pl.loop(1, spots)
-    def start_damp(offset):
-        send_f(1, offset).start()
-
-    own_f[1].start()
     for fetch in fetches[3:]:
         fetch.wait()
 
@@ -512,24 +507,26 @@
             (g_split[order, 0, block, :], g_split[order, 1, block, :]), (w_high[n], w_low[n])
         )
 
+    def slab_of(n):
+        return xbuf.at[pl.ds(n * spots, spots)]
+
     def arrive_u(turned):
         n = (here + n_tm - turned) % n_tm
 
-        @pl.loop(0, spots)
-        def wait_u(r):
-            slot = xbuf.at[n, r]
-            pltpu.make_async_copy(slot, slot, u_recv.at[n * spots + r]).wait()
-
-        solve_x_lines(n, 1, gathered(xbuf, lambda half: (n, slice(None), half)))
+        slot = slab_of(n)
+        pltpu.make_async_copy(slot, slot, u_recv.at[n]).wait()
+        solve_x_lines(n, 1, gathered(xbuf, lambda half: (pl.ds(n * spots, spots), half)))
         near_out[n] = leaving(n, 1, kept)
         send_near(n).start()
 
     pl.loop(1, n_tm // 2 + 1)(arrive_u)
-
-    @pl.loop(0, spots)
-    def wait_f(r):
-        slot = dbuf.at[0, r]
-        pltpu.make_async_copy(slot, slot, f_recv.at[0, r]).wait()
+    @pl.loop(1, spots)
+    def start_damp(offset):
+        send_f(1, offset).start()
+
+    own_f[1].start()
+
+    pltpu.make_async_copy(dbuf.at[0], dbuf.at[0], f_recv.at[0]).wait()
 
     source[1] = gathered(dbuf, lambda half: (0, slice(None), half)) * sea
     solve_x_lines(n_tm, 0, source[1])
@@ -538,14 +535,8 @@
 
     pl.loop(n_tm // 2 + 1, n_tm + 1)(arrive_u)
 
-    @pl.loop(0, n_tm)
-    def wait_p(n):
-        pltpu.make_async_copy(qbuf.at[n], qbuf.at[n], p_recv.at[n]).wait()
-
-    @pl.loop(0, spots)
-    def wait_damp(r):
-        slot = dbuf.at[1, r]
-        pltpu.make_async_copy(slot, slot, f_recv.at[1, r]).wait()
+    pltpu.make_async_copy(qbuf, qbuf, p_recv).wait()
+    pltpu.make_async_copy(dbuf.at[1], dbuf.at[1], f_recv.at[1]).wait()
 
     def wide(values):
         return jnp.concatenate([values[:1]] * halves, axis=1)
@@ -562,6 +553,12 @@
     def wait_near(n):
         pltpu.make_async_copy(near_in.at[n], near_in.at[n], near_recv.at[n]).wait()
 
+    away = xbuf.at[pl.ds(0, count - 1)]
+    pltpu.make_async_copy(away, away, u_send).wait()
+    away = dbuf.at[:, pl.ds(0, spots - 1)]
+    pltpu.make_async_copy(away, away, f_send).wait()
+    away = qbuf.at[pl.ds(0, n_tm - 1)]
+    pltpu.make_async_copy(away, away, p_send).wait()
     wait_near(n_tm)
     source[0] = joined(n_tm, 0)
 
@@ -576,7 +573,7 @@
     def finish_first(turned):
         n = (here + n_tm - turned) % n_tm
         wait_near(n)
-        field = gathered(xbuf, lambda half: (n, slice(None), half))
+        field = gathered(xbuf, lambda half: (pl.ds(n * spots, spots), half))
         state[n] = joined(n, 1) + offset_ref[n] - factor[n] * field
 
     @pl.loop(0, spots)
@@ -608,6 +605,8 @@
         @pl.loop(0, n_tm)
         def start_last(n):
             send_last(n, half).start()
+
+    pltpu.make_async_copy(near_in, near_in, near_send).wait()
 
     for half in range(halves):
 
@@ -642,7 +641,7 @@
                 total = factors[n] * total + offsets[n]
             fresh = total * inverse_p[block, lanes(half)]
             for n in range(n_tm):
-                obuf[half, n, r] = fresh
+                obuf[half * count + n * spots + r] = fresh
                 fresh = factors[n] * fresh + offsets[n]
             for n in range(n_tm):
 
@@ -651,44 +650,37 @@
                     send_o(half, n * spots + r).start()
 
         pltpu.make_async_copy(
-            obuf.at[half, here, spot], rbuf.at[half, my_t, chunk_rows(my_k), :], o_recv.at[half, me]
+            obuf.at[half * count + me], out_ref.at[my_t, half, chunk_rows(my_k), :], o_recv
         ).start()
 
-    for half in range(halves):
-        for t in range(n_t):
-
-            @pl.loop(t * per, (t + 1) * per)
-            def wait_o(index):
-                slot = rbuf.at[half, t, chunk_rows(index % per), :]
-                pltpu.make_async_copy(slot, slot, o_recv.at[half, index]).wait()
-
-            for y in range(rows):
-                part = rbuf[half, t, pl.ds(y, nz, stride=rows), :]
-                out_ref[t, pl.ds(half * LANES * rows + y, LANES, stride=rows), :] = part.T
-
-    @pl.loop(1, count)
-    def sent(offset):
-        send_u(offset).wait_send()
-        for half in range(halves):
-            send_o(half, (me + offset) % count).wait_send()
-
-    @pl.loop(1, spots)
-    def sent_f(offset):
-        for which in range(2):
-            send_f(which, offset).wait_send()
-
-    @pl.loop(1, n_tm)
-    def sent_p(offset):
-        send_p(offset).wait_send()
-
-    @pl.loop(0, n_tm + 1)
-    def sent_near(n):
-        send_near(n).wait_send()
-
-    @pl.loop(0, n_tm)
-    def sent_last(n):
-        for half in range(halves):
-            send_last(n, half).wait_send()
+    pltpu.make_async_copy(last_in, last_in, last_send).wait()
+    pltpu.make_async_copy(out_ref, out_ref, o_recv).wait()
+    away = obuf.at[pl.ds(0, halves * (count - 1))]
+    pltpu.make_async_copy(away, away, o_send).wait()
+
+
+def turn_kernel(size, in_ref, out_ref, near_ref, turned_ref, in_sem, out_sem):
+    n_t, halves, rows, nz = size
+    blocks = [(t, half) for half in range(halves) for t in range(n_t)]
+
+    def fetch(i):
+        return pltpu.make_async_copy(in_ref.at[blocks[i]], near_ref.at[i], in_sem.at[i])
+
+    def store(i):
+        t, half = blocks[i]
+        place = pl.ds(half * LANES * rows, LANES * rows)
+        return pltpu.make_async_copy(turned_ref.at[i], out_ref.at[t, place, :], out_sem.at[i])
+
+    for i in range(len(blocks)):
+        fetch(i).start()
+    for i in range(len(blocks)):
+        fetch(i).wait()
+        for y in range(rows):
+            part = near_ref[i, pl.ds(y, nz, stride=rows), :]
+            turned_ref[i, pl.ds(y, LANES, stride=rows), :] = part.T
+        store(i).start()
+    for i in range(len(blocks)):
+        store(i).wait()
 
 
 def whole_period(init_states, forcing, damp, kappa_x, kappa_y, kappa_z, sea_tiles, phases):
@@ -705,14 +697,13 @@
     tail, kept = 2 * chunk, 2 * (chunk + HALO)
     ext = LANES * -(-(all_rows + kept) // LANES)
     flat = (n_t, nx * rows, nz)
-    vmem = pl.BlockSpec(memory_space=pltpu.VMEM)
     f32 = jnp.float32
     bf16 = jnp.bfloat16
-    out = pl.pallas_call(
+    landed = pl.pallas_call(
         functools.partial(period_kernel, (n_tm, n_sp, n_t, nx, rows, nz)),
-        out_shape=jax.ShapeDtypeStruct(flat, f32),
+        out_shape=jax.ShapeDtypeStruct((n_t, halves, nz * rows, LANES), f32),
         in_specs=[pl.BlockSpec(memory_space=pltpu.HBM)] * 7 + [pl.BlockSpec(memory_space=pltpu.SMEM)],
-        out_specs=vmem,
+        out_specs=pl.BlockSpec(memory_space=pltpu.HBM),
         scratch_shapes=[
             pltpu.VMEM(flat, f32),
             pltpu.VMEM(flat, f32),
@@ -733,11 +724,10 @@
             pltpu.VMEM((n_t, halves, nz * rows, LANES), f32),
             pltpu.VMEM((n_t, 2, halves, nz * rows, LANES), f32),
             pltpu.VMEM((8, LANES), f32),
-            pltpu.VMEM((n_tm, spots, halves, wrows, LANES), f32),
+            pltpu.VMEM((count, halves, wrows, LANES), f32),
             pltpu.VMEM((2, spots, halves, wrows, LANES), f32),
             pltpu.VMEM((n_tm, 8, LANES), f32),
-            pltpu.VMEM((halves, n_tm, spots, crows, LANES), f32),
-            pltpu.VMEM((halves, n_t, nz * rows, LANES), f32),
+            pltpu.VMEM((halves * count, crows, LANES), f32),
             pltpu.VMEM((n_tm, all_rows, nx), f32),
             pltpu.VMEM((n_tm, all_rows, nx), f32),
             pltpu.VMEM((2, all_rows, nx), f32),
@@ -746,17 +736,17 @@
             pltpu.VMEM((n_tm + 1, kept, nx), f32),
             pltpu.VMEM((n_tm, halves, tail, LANES), f32),
             pltpu.VMEM((n_tm, halves, tail, LANES), f32),
-            pltpu.SemaphoreType.DMA((count,)),
-            pltpu.SemaphoreType.DMA((count,)),
-            pltpu.SemaphoreType.DMA((2, spots)),
-            pltpu.SemaphoreType.DMA((2, spots)),
+            pltpu.SemaphoreType.DMA,
             pltpu.SemaphoreType.DMA((n_tm,)),
-            pltpu.SemaphoreType.DMA((n_tm,)),
-            pltpu.SemaphoreType.DMA((halves, count)),
-            pltpu.SemaphoreType.DMA((halves, count)),
+            pltpu.SemaphoreType.DMA,
+            pltpu.SemaphoreType.DMA((2,)),
+            pltpu.SemaphoreType.DMA,
+            pltpu.SemaphoreType.DMA,
+            pltpu.SemaphoreType.DMA,
+            pltpu.SemaphoreType.DMA,
+            pltpu.SemaphoreType.DMA,
             pltpu.SemaphoreType.DMA((n_tm + 1,)),
-            pltpu.SemaphoreType.DMA((n_tm + 1,)),
-            pltpu.SemaphoreType.DMA((n_tm, halves)),
+            pltpu.SemaphoreType.DMA,
             pltpu.SemaphoreType.DMA((n_tm, halves)),
         ],
         compiler_params=pltpu.CompilerParams(
@@ -772,6 +762,19 @@
         sea_tiles.reshape(1, -1),
         phases,
     )
+    pieces = n_t * halves
+    out = pl.pallas_call(
+        functools.partial(turn_kernel, (n_t, halves, rows, nz)),
+        out_shape=jax.ShapeDtypeStruct(flat, f32),
+        in_specs=[pl.BlockSpec(memory_space=pl.ANY)],
+        out_specs=pl.BlockSpec(memory_space=pl.ANY),
+        scratch_shapes=[
+            pltpu.VMEM((pieces, nz * rows, LANES), f32),
+            pltpu.VMEM((pieces, LANES * rows, nz), f32),
+            pltpu.SemaphoreType.DMA((pieces,)),
+            pltpu.SemaphoreType.DMA((pieces,)),
+        ],
+    )(landed)
     return out.reshape(init_states.shape)
 
 

time: 44.5 us -> 42.6 us (0.957)
  local copies, waits for them, and re-layouts: 1.87 us -> 0 us
    pallas_call x0 -> x1, Pallas kernels: none -> 2.03 us  [whole_period(): pl.pallas_call(functools.partial(turn_kernel, (n_t, halves, rows, nz)), o...]
    pallas_call x1, Pallas kernels: 41.7 us -> 39.7 us  [whole_period(): pl.pallas_call(functools.partial(period_kernel, (n_tm, n_sp, n_t, nx, row...]
    unnamed x1 -> x0, local copies, waits for them, and re-layouts: 1.87 us -> none
where the time goes in v2:
time: 42.6 us; the launch traced here: 42.4 us
  Pallas kernels  41.8 us (98%)
  between operations  0.66 us (2%)
    pallas_call x1, Pallas kernels, whole_period(): pl.pallas_call(functools.partial(period_kernel, (n_tm, n_sp, n_t, nx, row...  39.7 us
    pallas_call x1, Pallas kernels, whole_period(): pl.pallas_call(functools.partial(turn_kernel, (n_t, halves, rows, nz)), o...  2.03 us

profile of v2, /device:TPU:0, one launch (start us, length us, event | category | flops | bytes accessed | tf_op | source)
XLA Modules:
  0.0 42.4 jit_solution(17328599187971923164)
XLA Ops:
  0.7 39.7 %shard_map.82.in_ref = f32[2,2,256,128]{3,2,1,0:T(8,128)} custom-call(f32[2,512,128]{2,1,0:T(8,128)} %bitcast.10, f32[2,512,128]{2,1,0:T(8,128)} %bitcast.11, f32[2,512,128]{2,1,0:T(8,128)} %bitcast.12, f32[1,256]{1,0:T(1,128)} %bitcast.13, f32[1,16]{1,0:T(1,128)} %bitcast.14, f32[1,128]{1,0:T(1,128)} %bitcast.15, s32[1,16]{1,0:T(1,128)} %bitcast.16, ...), custom_call_target="tpu_custom_call" | custom-call | tf_op jit(solution)/shard_map/pallas_call | solution.py:702
  40.4 2.0 %shard_map.83 = f32[2,512,128]{2,1,0:T(8,128)} custom-call(f32[2,2,256,128]{3,2,1,0:T(8,128)} %shard_map.82.in_ref), custom_call_target="tpu_custom_call" | custom-call | tf_op jit(solution)/shard_map/pallas_call | solution.py:766

commit v3 on v2

--- a/solution.py
+++ b/solution.py
@@ -120,6 +120,7 @@
 
 LANES = 128
 HALO = 2 * ITERS
+GROUPS = 1
 MESH = pl.DeviceIdType.MESH
 
 
@@ -134,7 +135,9 @@
 
 def dot3(a, b):
     once = functools.partial(jnp.dot, preferred_element_type=jnp.float32)
-    return once(a[0], b[0]) + (once(a[0], b[1]) + once(a[1], b[0]))
+    lines = a[0].shape[0]
+    both = once(jnp.concatenate(a, axis=0), b[0])
+    return both[:lines] + (once(a[0], b[1]) + both[lines:])
 
 
 def iota(shape, axis):
@@ -191,9 +194,9 @@
 
 
 def period_kernel(
-    size, u_hbm, f_hbm, damp_hbm, kx_hbm, ky_hbm, kz_hbm, sea_hbm, phase_ref, out_ref,
-    u_ref, f_ref, damp_ref, kx_ref, ky_ref, kz_ref, sea_ref, fetched, inverse_p,
-    g_split, a_split, g_ref, a_ref, w_high, w_low, ends,
+    size, u_hbm, f_hbm, damp_hbm, kx_hbm, ky_hbm, kz_hbm, sea_hbm, phase_hbm, out_ref,
+    u_ref, f_ref, damp_ref, kx_ref, ky_ref, kz_ref, sea_ref, phase_ref, fetched, inverse_p,
+    g_split, a_split, g_ref, a_ref, w_high, w_low, mix, ends,
     ubuf, fbuf, pbuf, xbuf, dbuf, qbuf, obuf, state, factor, source, offset_ref,
     near_out, near_in, last_out, last_in,
     u_send, u_recv, f_send, f_recv, p_send, p_recv, o_send, o_recv,
@@ -212,6 +215,8 @@
     tail, kept = 2 * chunk, 2 * (chunk + HALO)
     ext = LANES * -(-(all_rows + kept) // LANES)
     ny = n_sp * rows
+    pieces = [(half, group) for half in range(halves) for group in range(GROUPS)]
+    prows = crows // GROUPS
 
     here = lax.axis_index("tm")
     space = lax.axis_index("space")
@@ -239,6 +244,7 @@
         (ky_hbm, ky_ref),
         (kz_hbm, kz_ref),
         (sea_hbm, sea_ref),
+        (phase_hbm, phase_ref),
     )
     fetches = [
         pltpu.make_async_copy(far, near, fetched.at[i]) for i, (far, near) in enumerate(pairs)
@@ -263,7 +269,8 @@
                     part = ref[t, pl.ds(half * LANES * rows + y, LANES, stride=rows), :]
                     buf[(t, *where, half, pl.ds(y, nz, stride=rows), slice(None))] = part.T
 
-    pbuf[...] = jnp.full((8, LANES), phase_ref[0].astype(jnp.float32))
+    fetches[7].wait()
+    pbuf[...] = jnp.broadcast_to(phase_ref[...].astype(jnp.float32), (8, LANES))
 
     my_t, my_k = me // per, me % per
     my_start = window_start(my_k)
@@ -282,7 +289,7 @@
     own_p = pltpu.make_async_copy(pbuf, qbuf.at[here], p_recv)
 
     def send_u(offset):
-        index = (me + offset) % count
+        index = (here ^ (offset // spots)) * spots + (spot ^ (offset % spots))
         return pltpu.make_async_remote_copy(
             src_ref=ubuf.at[index // per, :, window_rows(index % per), :],
             dst_ref=xbuf.at[here * spots + spot],
@@ -323,20 +330,25 @@
             device_id_type=MESH,
         )
 
-    def send_last(n, half):
+    def send_last(n, piece):
         return pltpu.make_async_remote_copy(
-            src_ref=last_out.at[n, half],
-            dst_ref=last_in.at[n, half],
+            src_ref=last_out.at[piece, n],
+            dst_ref=last_in.at[piece, n],
             send_sem=last_send,
-            recv_sem=last_recv.at[n, half],
+            recv_sem=last_recv.at[piece],
             device_id=across,
             device_id_type=MESH,
         )
 
-    def send_o(half, index):
+    def landing(piece):
+        half, group = pieces[piece]
+        place = pl.ds(pl.multiple_of(my_k * crows + group * prows, 8), prows)
+        return out_ref.at[my_t, half, place, :]
+
+    def send_o(piece, index):
         return pltpu.make_async_remote_copy(
-            src_ref=obuf.at[half * count + index],
-            dst_ref=out_ref.at[my_t, half, chunk_rows(my_k), :],
+            src_ref=obuf.at[piece * count + index],
+            dst_ref=landing(piece),
             send_sem=o_send,
             recv_sem=o_recv,
             device_id=device(index),
@@ -351,8 +363,7 @@
     def start_p(offset):
         send_p(offset).start()
 
-    @pl.loop(1, count // 2 + 1)
-    def start_u(offset):
+    for offset in (11, 10, 9, 8, 15, 14, 13, 12):
         send_u(offset).start()
 
     own_p.start()
@@ -366,14 +377,13 @@
 
     own_f[0].start()
 
-    @pl.loop(count // 2 + 1, count)
-    def start_u_rest(offset):
+    for offset in (7, 6, 5, 4, 3, 2, 1):
         send_u(offset).start()
 
     fetches[2].wait()
     turn(damp_ref, fbuf, (1,))
 
-    for fetch in fetches[3:]:
+    for fetch in fetches[3:7]:
         fetch.wait()
 
     for half, block in enumerate(reduced_inverse(kx_ref[...], nx)):
@@ -464,10 +474,16 @@
     def inner_rows(r):
         return pl.ds(pl.multiple_of(r * wrows + inner, 8), crows)
 
-    for i, part in enumerate(
-        parts(jnp.concatenate([g_ref[inner_rows(r), :] for r in range(spots)], axis=0))
-    ):
+    inner_g = jnp.concatenate([g_ref[inner_rows(r), :] for r in range(spots)], axis=0)
+    inner_g = jnp.where(iota((spots * crows, ext), 1) < all_rows, inner_g, 0.0)
+    for i, part in enumerate(parts(inner_g)):
         g_split[2, i, : spots * crows, :] = part
+    q = iota((spots * prows, LANES), 0)
+    picked = side * (ny // 2) + (q // prows) * rows + q % rows
+    picked = jnp.where(picked == iota((spots * prows, LANES), 1), 1.0, 0.0)[:, :ny]
+    enters = [dot(picked, jnp.broadcast_to(c, (ny, LANES))) for c in (enter_twice, enter_once)]
+    mix[0] = jnp.where(q % 2 == 0, enters[0], enters[1])
+    mix[1] = jnp.where(q % 2 == 0, enters[1], enters[0])
 
     w_high[:, all_rows:, :] = jnp.zeros((n_tm + 1, ext - all_rows, nx), jnp.bfloat16)
     w_low[:, all_rows:, :] = jnp.zeros((n_tm + 1, ext - all_rows, nx), jnp.bfloat16)
@@ -511,7 +527,7 @@
         return xbuf.at[pl.ds(n * spots, spots)]
 
     def arrive_u(turned):
-        n = (here + n_tm - turned) % n_tm
+        n = here ^ ((turned + 1) % n_tm)
 
         slot = slab_of(n)
         pltpu.make_async_copy(slot, slot, u_recv.at[n]).wait()
@@ -571,7 +587,7 @@
 
     @pl.loop(1, n_tm + 1)
     def finish_first(turned):
-        n = (here + n_tm - turned) % n_tm
+        n = here ^ ((turned + 1) % n_tm)
         wait_near(n)
         field = gathered(xbuf, lambda half: (pl.ds(n * spots, spots), half))
         state[n] = joined(n, 1) + offset_ref[n] - factor[n] * field
@@ -592,70 +608,81 @@
     def lanes(half):
         return slice(half * LANES, (half + 1) * LANES)
 
-    @pl.loop(0, n_tm)
-    def leave_last(n):
+    first_pieces = 1
+
+    for n in range(n_tm):
         solve_x_lines(n, 1, state[n])
+    for n in range(n_tm):
         found = leaving(n, 1, tail)
-        for half in range(halves):
-            last_out[n, half] = found[:, lanes(half)]
-        send_last(n, 0).start()
-
-    for half in range(1, halves):
+        for piece, (half, group) in enumerate(pieces):
+            last_out[piece, n] = found[group * prows : (group + 1) * prows, lanes(half)]
+        for piece in range(first_pieces):
+            send_last(n, piece).start()
+
+    for piece in range(first_pieces, len(pieces)):
 
         @pl.loop(0, n_tm)
         def start_last(n):
-            send_last(n, half).start()
+            send_last(n, piece).start()
 
     pltpu.make_async_copy(near_in, near_in, near_send).wait()
 
-    for half in range(halves):
-
-        @pl.loop(0, n_tm)
-        def finish_last(n):
-            slot = last_in.at[n, half]
-            pltpu.make_async_copy(slot, slot, last_recv.at[n, half]).wait()
-            block = slice(all_rows, all_rows + tail)
-            high, low = parts(last_in[n, half])
-            w_high[n, block, lanes(half)] = high
-            w_low[n, block, lanes(half)] = low
-            upper = slice(0, spots * crows)
-            ends[n] = dot3(
-                (g_split[2, 0, upper, :], g_split[2, 1, upper, :]),
-                (w_high[n, :, lanes(half)], w_low[n, :, lanes(half)]),
+    @pl.loop(0, n_tm)
+    def own_last(n):
+        upper = slice(0, spots * crows)
+        own = dot3(
+            (g_split[2, 0, upper, :], g_split[2, 1, upper, :]), (w_high[n], w_low[n])
+        )
+        for r in range(spots):
+            packed = slice(r * crows, (r + 1) * crows)
+            block = inner_rows(r)
+            ends[n, packed, :] = (
+                own[packed] + offset_ref[n, block, :] - factor[n, block, :] * state[n, block, :]
             )
 
-        @pl.loop(1, spots + 1)
+    even = iota((prows, LANES), 0) % 2 == 0
+
+    def swapped(a):
+        return jnp.where(even, pltpu.roll(a, prows - 1, 0), pltpu.roll(a, 1, 0))
+
+    for piece, (half, group) in enumerate(pieces):
+        slot = last_in.at[piece]
+        pltpu.make_async_copy(slot, slot, last_recv.at[piece]).wait()
+
         def solve_last(turned):
             r = (spot + turned) % spots
-            block = inner_rows(r)
-            packed = pl.ds(pl.multiple_of(r * crows, 8), crows)
+            block = pl.ds(pl.multiple_of(r * wrows + inner + group * prows, 8), prows)
+            packed = pl.ds(pl.multiple_of(r * crows + group * prows, 8), prows)
+            mine = pl.ds(pl.multiple_of(r * prows, 8), prows)
             factors = [factor[n, block, lanes(half)] for n in range(n_tm)]
-            offsets = [
-                ends[n, packed, :]
-                + offset_ref[n, block, lanes(half)]
-                - factors[n] * state[n, block, lanes(half)]
-                for n in range(n_tm)
-            ]
+            offsets = []
+            for n in range(n_tm):
+                entering = last_in[piece, n]
+                offsets.append(
+                    ends[n, packed, lanes(half)]
+                    + mix[0, mine, :] * entering
+                    + mix[1, mine, :] * swapped(entering)
+                )
             total = offsets[0]
             for n in range(1, n_tm):
                 total = factors[n] * total + offsets[n]
             fresh = total * inverse_p[block, lanes(half)]
             for n in range(n_tm):
-                obuf[half * count + n * spots + r] = fresh
+                obuf[piece * count + n * spots + r] = fresh
                 fresh = factors[n] * fresh + offsets[n]
             for n in range(n_tm):
 
                 @pl.when(n * spots + r != me)
                 def _():
-                    send_o(half, n * spots + r).start()
-
-        pltpu.make_async_copy(
-            obuf.at[half * count + me], out_ref.at[my_t, half, chunk_rows(my_k), :], o_recv
-        ).start()
+                    send_o(piece, n * spots + r).start()
+
+        for turned in range(1, spots + 1):
+            solve_last(turned)
+        pltpu.make_async_copy(obuf.at[piece * count + me], landing(piece), o_recv).start()
 
     pltpu.make_async_copy(last_in, last_in, last_send).wait()
     pltpu.make_async_copy(out_ref, out_ref, o_recv).wait()
-    away = obuf.at[pl.ds(0, halves * (count - 1))]
+    away = obuf.at[pl.ds(0, len(pieces) * (count - 1))]
     pltpu.make_async_copy(away, away, o_send).wait()
 
 
@@ -694,7 +721,8 @@
     wrows = window * rows
     crows = chunk * rows
     all_rows = spots * wrows
-    tail, kept = 2 * chunk, 2 * (chunk + HALO)
+    kept = 2 * (chunk + HALO)
+    prows = crows // GROUPS
     ext = LANES * -(-(all_rows + kept) // LANES)
     flat = (n_t, nx * rows, nz)
     f32 = jnp.float32
@@ -702,7 +730,7 @@
     landed = pl.pallas_call(
         functools.partial(period_kernel, (n_tm, n_sp, n_t, nx, rows, nz)),
         out_shape=jax.ShapeDtypeStruct((n_t, halves, nz * rows, LANES), f32),
-        in_specs=[pl.BlockSpec(memory_space=pltpu.HBM)] * 7 + [pl.BlockSpec(memory_space=pltpu.SMEM)],
+        in_specs=[pl.BlockSpec(memory_space=pltpu.HBM)] * 8,
         out_specs=pl.BlockSpec(memory_space=pltpu.HBM),
         scratch_shapes=[
             pltpu.VMEM(flat, f32),
@@ -712,7 +740,8 @@
             pltpu.VMEM((1, kappa_y.shape[0]), f32),
             pltpu.VMEM((1, nz), f32),
             pltpu.VMEM((1, sea_tiles.shape[0]), jnp.int32),
-            pltpu.SemaphoreType.DMA((7,)),
+            pltpu.VMEM((1, 1), jnp.int32),
+            pltpu.SemaphoreType.DMA((8,)),
             pltpu.VMEM((all_rows, nx), f32),
             pltpu.VMEM((3, 2, ext, ext), bf16),
             pltpu.VMEM((2, 2, nx, nx), bf16),
@@ -720,22 +749,23 @@
             pltpu.VMEM((nx, nx), f32),
             pltpu.VMEM((n_tm + 1, ext, nx), bf16),
             pltpu.VMEM((n_tm + 1, ext, nx), bf16),
-            pltpu.VMEM((n_tm, spots * crows, LANES), f32),
+            pltpu.VMEM((2, spots * prows, LANES), f32),
+            pltpu.VMEM((n_tm, spots * crows, nx), f32),
             pltpu.VMEM((n_t, halves, nz * rows, LANES), f32),
             pltpu.VMEM((n_t, 2, halves, nz * rows, LANES), f32),
             pltpu.VMEM((8, LANES), f32),
             pltpu.VMEM((count, halves, wrows, LANES), f32),
             pltpu.VMEM((2, spots, halves, wrows, LANES), f32),
             pltpu.VMEM((n_tm, 8, LANES), f32),
-            pltpu.VMEM((halves * count, crows, LANES), f32),
+            pltpu.VMEM((halves * GROUPS * count, prows, LANES), f32),
             pltpu.VMEM((n_tm, all_rows, nx), f32),
             pltpu.VMEM((n_tm, all_rows, nx), f32),
             pltpu.VMEM((2, all_rows, nx), f32),
             pltpu.VMEM((n_tm, all_rows, nx), f32),
             pltpu.VMEM((n_tm + 1, kept, nx), f32),
             pltpu.VMEM((n_tm + 1, kept, nx), f32),
-            pltpu.VMEM((n_tm, halves, tail, LANES), f32),
-            pltpu.VMEM((n_tm, halves, tail, LANES), f32),
+            pltpu.VMEM((halves * GROUPS, n_tm, prows, LANES), f32),
+            pltpu.VMEM((halves * GROUPS, n_tm, prows, LANES), f32),
             pltpu.SemaphoreType.DMA,
             pltpu.SemaphoreType.DMA((n_tm,)),
             pltpu.SemaphoreType.DMA,
@@ -747,7 +777,7 @@
             pltpu.SemaphoreType.DMA,
             pltpu.SemaphoreType.DMA((n_tm + 1,)),
             pltpu.SemaphoreType.DMA,
-            pltpu.SemaphoreType.DMA((n_tm, halves)),
+            pltpu.SemaphoreType.DMA((halves * GROUPS,)),
         ],
         compiler_params=pltpu.CompilerParams(
             collective_id=0, has_side_effects=True, vmem_limit_bytes=63 * 1024 * 1024
@@ -760,7 +790,7 @@
         kappa_y[None],
         kappa_z[None],
         sea_tiles.reshape(1, -1),
-        phases,
+        phases.reshape(1, 1),
     )
     pieces = n_t * halves
     out = pl.pallas_call(
@@ -795,7 +825,8 @@
         and nz == LANES
         and nx % LANES == 0
         and nz % per == 0
-        and chunk * rows % 8 == 0
+        and rows == 2
+        and chunk * rows % (8 * GROUPS) == 0
         and HALO * rows % 8 == 0
         and HALO <= chunk
         and chunk % 8 == 0

time: 42.6 us -> 41.1 us (0.965)
  Pallas kernels: 41.8 us -> 40.2 us
    pallas_call x1, Pallas kernels: 39.7 us -> 38.2 us  [whole_period(): pl.pallas_call(functools.partial(period_kernel, (n_tm, n_sp, n_t, nx, row...]
where the time goes in v3:
time: 41.1 us; the launch traced here: 40.9 us
  Pallas kernels  40.2 us (98%)
  between operations  0.66 us (2%)
    pallas_call x1, Pallas kernels, whole_period(): pl.pallas_call(functools.partial(period_kernel, (n_tm, n_sp, n_t, nx, row...  38.2 us
    pallas_call x1, Pallas kernels, whole_period(): pl.pallas_call(functools.partial(turn_kernel, (n_t, halves, rows, nz)), o...  2.03 us

profile of v3, /device:TPU:0, one launch (start us, length us, event | category | flops | bytes accessed | tf_op | source)
XLA Modules:
  0.0 40.9 jit_solution(6473764157009649984)
XLA Ops:
  0.7 38.2 %shard_map.82.in_ref = f32[2,2,256,128]{3,2,1,0:T(8,128)} custom-call(f32[2,512,128]{2,1,0:T(8,128)} %bitcast.12, f32[2,512,128]{2,1,0:T(8,128)} %bitcast.13, f32[2,512,128]{2,1,0:T(8,128)} %bitcast.14, f32[1,256]{1,0:T(1,128)} %bitcast.15, f32[1,16]{1,0:T(1,128)} %bitcast.16, f32[1,128]{1,0:T(1,128)} %bitcast.17, s32[1,16]{1,0:T(1,128)} %bitcast.18, ...), custom_call_target="tpu_custom_call" | custom-call | tf_op jit(solution)/shard_map/pallas_call | solution.py:730
  38.9 2.0 %shard_map.83 = f32[2,512,128]{2,1,0:T(8,128)} custom-call(f32[2,2,256,128]{3,2,1,0:T(8,128)} %shard_map.82.in_ref), custom_call_target="tpu_custom_call" | custom-call | tf_op jit(solution)/shard_map/pallas_call | solution.py:796

commit v4 on v3

--- a/solution.py
+++ b/solution.py
@@ -300,7 +300,7 @@
         )
 
     def send_f(which, offset):
-        index = here * spots + (spot + offset) % spots
+        index = here * spots + (spot ^ (spots - offset))
         return pltpu.make_async_remote_copy(
             src_ref=fbuf.at[index // per, which, :, window_rows(index % per), :],
             dst_ref=dbuf.at[which, spot],
@@ -363,7 +363,13 @@
     def start_p(offset):
         send_p(offset).start()
 
-    for offset in (11, 10, 9, 8, 15, 14, 13, 12):
+    far_first = [
+        pair * spots + step
+        for pair in (2, 3, 1, 0)
+        for step in reversed(range(spots))
+        if pair + step > 0
+    ]
+    for offset in far_first[: count // 2]:
         send_u(offset).start()
 
     own_p.start()
@@ -377,7 +383,7 @@
 
     own_f[0].start()
 
-    for offset in (7, 6, 5, 4, 3, 2, 1):
+    for offset in far_first[count // 2 :]:
         send_u(offset).start()
 
     fetches[2].wait()
@@ -535,12 +541,15 @@
         near_out[n] = leaving(n, 1, kept)
         send_near(n).start()
 
-    pl.loop(1, n_tm // 2 + 1)(arrive_u)
+    arrive_u(1)
+
     @pl.loop(1, spots)
     def start_damp(offset):
         send_f(1, offset).start()
 
     own_f[1].start()
+
+    arrive_u(2)
 
     pltpu.make_async_copy(dbuf.at[0], dbuf.at[0], f_recv.at[0]).wait()
 
@@ -592,7 +601,6 @@
         field = gathered(xbuf, lambda half: (pl.ds(n * spots, spots), half))
         state[n] = joined(n, 1) + offset_ref[n] - factor[n] * field
 
-    @pl.loop(0, spots)
     def solve_first(r):
         block = pl.ds(pl.multiple_of(r * wrows, 8), wrows)
         factors = [factor[n, block, :] for n in range(n_tm)]
@@ -605,17 +613,24 @@
             state[n, block, :] = fresh
             fresh = factors[n] * fresh + offsets[n]
 
+    for r in range(spots):
+        solve_first(r)
+
     def lanes(half):
         return slice(half * LANES, (half + 1) * LANES)
 
     first_pieces = 1
 
+    a_twice = a_split[1, 0], a_split[1, 1]
+    picked_rows = []
     for n in range(n_tm):
-        solve_x_lines(n, 1, state[n])
+        w_high[n, :all_rows, :], w_low[n, :all_rows, :] = parts(state[n])
+        picked_rows.append(leaving(n, 1, tail))
+    found = dot3(parts(jnp.concatenate(picked_rows, axis=0)), a_twice)
     for n in range(n_tm):
-        found = leaving(n, 1, tail)
         for piece, (half, group) in enumerate(pieces):
-            last_out[piece, n] = found[group * prows : (group + 1) * prows, lanes(half)]
+            first = n * tail + group * prows
+            last_out[piece, n] = found[first : first + prows, lanes(half)]
         for piece in range(first_pieces):
             send_last(n, piece).start()
 
@@ -627,18 +642,21 @@
 
     pltpu.make_async_copy(near_in, near_in, near_send).wait()
 
-    @pl.loop(0, n_tm)
     def own_last(n):
         upper = slice(0, spots * crows)
         own = dot3(
             (g_split[2, 0, upper, :], g_split[2, 1, upper, :]), (w_high[n], w_low[n])
         )
+        own = dot3(parts(own), a_twice)
         for r in range(spots):
             packed = slice(r * crows, (r + 1) * crows)
             block = inner_rows(r)
             ends[n, packed, :] = (
                 own[packed] + offset_ref[n, block, :] - factor[n, block, :] * state[n, block, :]
             )
+
+    for n in range(n_tm):
+        own_last(n)
 
     even = iota((prows, LANES), 0) % 2 == 0
 
@@ -820,7 +838,8 @@
         ITERS == 2
         and slabs == 1
         and lax.axis_size("space") % 2 == 0
-        and lax.axis_size("tm") % 2 == 0
+        and lax.axis_size("tm") == 4
+        and spots & (spots - 1) == 0
         and count % n_t == 0
         and nz == LANES
         and nx % LANES == 0

time: 41.1 us -> 40.3 us (0.981)
  Pallas kernels: 40.2 us -> 39.5 us
    pallas_call x1, Pallas kernels: 38.2 us -> 37.4 us  [whole_period(): pl.pallas_call(functools.partial(period_kernel, (n_tm, n_sp, n_t, nx, row...]
where the time goes in v4:
time: 40.3 us; the launch traced here: 40.1 us
  Pallas kernels  39.5 us (98%)
  between operations  0.66 us (2%)
    pallas_call x1, Pallas kernels, whole_period(): pl.pallas_call(functools.partial(period_kernel, (n_tm, n_sp, n_t, nx, row...  37.4 us
    pallas_call x1, Pallas kernels, whole_period(): pl.pallas_call(functools.partial(turn_kernel, (n_t, halves, rows, nz)), o...  2.03 us

profile of v4, /device:TPU:0, one launch (start us, length us, event | category | flops | bytes accessed | tf_op | source)
XLA Modules:
  0.0 40.1 jit_solution(12066500267998570937)
XLA Ops:
  0.7 37.4 %shard_map.82.in_ref = f32[2,2,256,128]{3,2,1,0:T(8,128)} custom-call(f32[2,512,128]{2,1,0:T(8,128)} %bitcast.12, f32[2,512,128]{2,1,0:T(8,128)} %bitcast.13, f32[2,512,128]{2,1,0:T(8,128)} %bitcast.14, f32[1,256]{1,0:T(1,128)} %bitcast.15, f32[1,16]{1,0:T(1,128)} %bitcast.16, f32[1,128]{1,0:T(1,128)} %bitcast.17, s32[1,16]{1,0:T(1,128)} %bitcast.18, ...), custom_call_target="tpu_custom_call" | custom-call | tf_op jit(solution)/shard_map/pallas_call | solution.py:748
  38.1 2.0 %shard_map.83 = f32[2,512,128]{2,1,0:T(8,128)} custom-call(f32[2,2,256,128]{3,2,1,0:T(8,128)} %shard_map.82.in_ref), custom_call_target="tpu_custom_call" | custom-call | tf_op jit(solution)/shard_map/pallas_call | solution.py:814

commit v5 on v4

--- a/solution.py
+++ b/solution.py
@@ -537,9 +537,12 @@
 
         slot = slab_of(n)
         pltpu.make_async_copy(slot, slot, u_recv.at[n]).wait()
-        solve_x_lines(n, 1, gathered(xbuf, lambda half: (pl.ds(n * spots, spots), half)))
-        near_out[n] = leaving(n, 1, kept)
+        field = parts(gathered(xbuf, lambda half: (pl.ds(n * spots, spots), half)))
+        w_high[n, :all_rows, :], w_low[n, :all_rows, :] = field
+        a_twice = a_split[1, 0], a_split[1, 1]
+        near_out[n] = dot3(parts(leaving(n, 1, kept)), a_twice)
         send_near(n).start()
+        w_high[n, :all_rows, :], w_low[n, :all_rows, :] = parts(dot3(field, a_twice))
 
     arrive_u(1)
 
@@ -558,7 +561,8 @@
     near_out[n_tm] = leaving(n_tm, 0, kept)
     send_near(n_tm).start()
 
-    pl.loop(n_tm // 2 + 1, n_tm + 1)(arrive_u)
+    arrive_u(3)
+    arrive_u(4)
 
     pltpu.make_async_copy(qbuf, qbuf, p_recv).wait()
     pltpu.make_async_copy(dbuf.at[1], dbuf.at[1], f_recv.at[1]).wait()

time: 40.3 us -> 40.3 us (level)
  no operation moved by 1% of the time
where the time goes in v5:
time: 40.3 us; the launch traced here: 40.1 us
  Pallas kernels  39.4 us (98%)
  between operations  0.66 us (2%)
    pallas_call x1, Pallas kernels, whole_period(): pl.pallas_call(functools.partial(period_kernel, (n_tm, n_sp, n_t, nx, row...  37.4 us
    pallas_call x1, Pallas kernels, whole_period(): pl.pallas_call(functools.partial(turn_kernel, (n_t, halves, rows, nz)), o...  2.03 us

profile of v5, /device:TPU:0, one launch (start us, length us, event | category | flops | bytes accessed | tf_op | source)
XLA Modules:
  0.0 40.1 jit_solution(3622646042681414605)
XLA Ops:
  0.7 37.4 %shard_map.82.in_ref = f32[2,2,256,128]{3,2,1,0:T(8,128)} custom-call(f32[2,512,128]{2,1,0:T(8,128)} %bitcast.12, f32[2,512,128]{2,1,0:T(8,128)} %bitcast.13, f32[2,512,128]{2,1,0:T(8,128)} %bitcast.14, f32[1,256]{1,0:T(1,128)} %bitcast.15, f32[1,16]{1,0:T(1,128)} %bitcast.16, f32[1,128]{1,0:T(1,128)} %bitcast.17, s32[1,16]{1,0:T(1,128)} %bitcast.18, ...), custom_call_target="tpu_custom_call" | custom-call | tf_op jit(solution)/shard_map/pallas_call | solution.py:752
  38.1 2.0 %shard_map.83 = f32[2,512,128]{2,1,0:T(8,128)} custom-call(f32[2,2,256,128]{3,2,1,0:T(8,128)} %shard_map.82.in_ref), custom_call_target="tpu_custom_call" | custom-call | tf_op jit(solution)/shard_map/pallas_call | solution.py:818
